TPU v7x, 256 devices: a whole 4x4x8 slice. The times are simulated.
256 devices in a mesh: seq: 8 (over y_lo, x), vocab: 32 (over z, y_hi, core).
Axes of the slice: x: 4, y: 4 (y_hi: 2, y_lo: 2; y = y_hi * 2 + y_lo), z: 8, core: 2. Of those that a mesh axis runs over, the one named last changes fastest.
Arguments:
- hidden: bfloat16 [8, 32, 2, 16, 2048], P('seq', 'vocab'), may hold values from -4 to 4
- head_weight: bfloat16 [32768, 2048], P('vocab'), may hold values from -4 to 4
- targets: int32 [8, 32, 2, 16], P('seq', 'vocab'), may hold values from 0 to 32767
- span_counts: int32 [8, 32, 2], P('seq', 'vocab'), may hold values from 0 to 16, as said below
- send_counts: int32 [8, 32, 8], P('seq', 'vocab'), may hold values from 0 to 4, as said below
Outputs:
- loss_rows: float32 [8, 32, 16], P('seq', 'vocab')
- hidden_grad: bfloat16 [8, 32, 2, 16, 2048], P('seq', 'vocab')
- code_grad: bfloat16 [32768, 2048], P('vocab', 'seq')
Inputs may be any that keep to these rules, and one draw needn't show every extreme that they name: `span_counts`: the two span counts of an owner sum to 16. `send_counts`: every entry is 0 or 4; each row owner receives exactly 16 rows in all; an owner's counts sum to the sum of its two span counts.
All inputs are finite; a program needn't handle non-finite values.
Results may differ from a plain program's by a relative error of at most 0.019.
Values may be sent and summed in bfloat16 or wider, within the bound.
A program may use at most 64 MiB of HBM per device.

v0:
```python
import jax
import jax.numpy as jnp
from jax import lax
from jax.sharding import PartitionSpec as P

loss_scale = 4.0


def dense_repacking(valid_entries, count_of_rows):
    live_flags = valid_entries.astype(jnp.int32)
    before = jnp.cumsum(live_flags) - live_flags
    target_row = jnp.arange(count_of_rows, dtype=jnp.int32)[:, None]
    return valid_entries[None, :] & (before[None, :] == target_row)


def head_step(block_rows, block_targets, weight):
    count_of_rows = block_rows.shape[0]
    vocab_width = weight.shape[0]
    all_rows, all_targets = (
        lax.all_gather(block_rows, "vocab", axis=0, tiled=True),
        lax.all_gather(block_targets, "vocab", axis=0, tiled=True),
    )
    logits = lax.dot_general(
        all_rows, weight, (((1,), (1,)), ((), ())), preferred_element_type=jnp.float32
    )
    local_target = all_targets - lax.axis_index("vocab") * vocab_width
    target_hit = local_target[:, None] == jnp.arange(vocab_width, dtype=jnp.int32)[None, :]
    target_part = jnp.sum(jnp.where(target_hit, logits, 0.0), axis=1)
    local_top = jnp.max(logits, axis=1)
    row_top = lax.pmax(local_top, "vocab")
    local_total = jnp.sum(jnp.exp(logits - row_top[:, None]), axis=1)
    row_total, target_logit = lax.psum((local_total, target_part), "vocab")
    log_total = row_top + jnp.log(row_total)
    valid_entries = all_targets >= 0
    logit_grads = jnp.where(
        valid_entries[:, None],
        loss_scale * (jnp.exp(logits - log_total[:, None]) - target_hit.astype(jnp.float32)),
        0.0,
    ).astype(jnp.bfloat16)
    own_start = lax.axis_index("vocab") * count_of_rows
    own_loss = lax.dynamic_slice_in_dim(
        jnp.where(valid_entries, log_total - target_logit, 0.0), own_start, count_of_rows
    )
    row_grad = lax.psum_scatter(
        jnp.dot(logit_grads, weight, preferred_element_type=jnp.float32).astype(jnp.bfloat16),
        "vocab",
        scatter_dimension=0,
        tiled=True,
    ).astype(jnp.float32)
    partial_value = lax.dot_general(
        logit_grads, all_rows, (((0,), (0,)), ((), ())), preferred_element_type=jnp.float32
    )
    code_grad = lax.psum_scatter(
        partial_value.astype(jnp.bfloat16), "seq", scatter_dimension=1, tiled=True
    )
    return (own_loss, row_grad, code_grad)


def per_device(hidden, head_weight, targets, span_counts, send_counts):
    window_len = hidden.shape[3]
    model_width = hidden.shape[4]
    count_of_slots = window_len // 4
    partner_device_count = lax.axis_size("seq")
    evened_row_layout = partner_device_count * count_of_slots // 2
    flat_rows = hidden.reshape(2 * window_len, model_width)
    sent_counts = send_counts.reshape(partner_device_count)
    span_sizes = span_counts.reshape(2)
    position = jnp.arange(2 * window_len, dtype=jnp.int32)
    in_first = position < window_len
    speech = jnp.where(
        in_first,
        position >= window_len - span_sizes[0],
        position - window_len >= window_len - span_sizes[1],
    )
    speech_rank = jnp.where(
        in_first,
        position - window_len + span_sizes[0],
        span_sizes[0] + position - 2 * window_len + span_sizes[1],
    )
    marked = jnp.where(speech, targets.reshape(2 * window_len), -1)
    offsets = jnp.cumsum(sent_counts) - sent_counts
    slot_index = jnp.arange(count_of_slots, dtype=jnp.int32)
    slot_rank = (offsets[:, None] + slot_index[None, :]).reshape(
        partner_device_count * count_of_slots
    )
    slot_live = (slot_index[None, :] < sent_counts[:, None]).reshape(
        partner_device_count * count_of_slots
    )
    placing = speech[:, None] & slot_live[None, :] & (speech_rank[:, None] == slot_rank[None, :])
    contract_rows = (((0,), (0,)), ((), ()))
    source_loss, row_grad, code_grad = head_step(flat_rows, marked, head_weight)
    source_grad = row_grad.astype(jnp.bfloat16)
    slot_loss = lax.dot_general(
        placing.astype(jnp.float32), source_loss, contract_rows, precision=lax.Precision.HIGHEST
    )
    arrived_loss, received_valid_flags = (
        lax.all_to_all(
            slot_loss.reshape(partner_device_count, count_of_slots),
            "seq",
            split_axis=0,
            concat_axis=0,
            tiled=True,
        ),
        lax.all_to_all(
            slot_live.astype(jnp.float32).reshape(partner_device_count, count_of_slots),
            "seq",
            split_axis=0,
            concat_axis=0,
            tiled=True,
        ),
    )
    packed_layout = dense_repacking(
        received_valid_flags.reshape(partner_device_count * count_of_slots) > 0.5, evened_row_layout
    )
    loss_rows = jnp.dot(
        packed_layout.astype(jnp.float32),
        arrived_loss.reshape(partner_device_count * count_of_slots),
        precision=lax.Precision.HIGHEST,
    )
    return (
        loss_rows.reshape(1, 1, evened_row_layout),
        source_grad.reshape(hidden.shape),
        code_grad,
    )


def solution(mesh):
    in_specs = (
        P("seq", "vocab", None, None, None),
        P("vocab", None),
        P("seq", "vocab", None, None),
        P("seq", "vocab", None),
        P("seq", "vocab", None),
    )
    out_specs = (P("seq", "vocab", None), P("seq", "vocab", None, None, None), P("vocab", "seq"))
    return jax.shard_map(
        per_device, mesh=mesh, in_specs=in_specs, out_specs=out_specs, check_vma=False
    )
```

profile of v0, /device:TPU:32, one launch (start us, length us, event | category | flops | bytes accessed | tf_op | source)
XLA Modules:
  0.0 445.4 jit_solution(17002286004664026150)
XLA Ops:
  7.2 0.7 all-gather.2.cloned.1.call-update
  8.0 0.8 reshape.217
  8.7 1.3 fusion.10
  11.2 1.3 dynamic-slice
  13.3 20.2 %all-reduce = s32[1024]{0:T(1024)S(1)} all-reduce(s32[1024]{0:T(1024)S(1)} %get-tuple-element.10), channel_id=1, replica_groups=mesh['seq'=8,'vocab'=32] {'vocab'}, use_global_device_ids=true, to_apply=%add | all-reduce | flops 1024 | bytes 8192
  33.5 66.2 %all-gather.2.cloned.1.call-done = bf16[1024,2048]{1,0:T(8,128)(2,1)} async-done(((bf16[32,2048]{1,0:T(8,128)(2,1)}), bf16[1024,2048]{1,0:T(8,128)(2,1)}) %all-gather.2.cloned.1.call-update) | async-done | bytes 4194320 | tf_op jit(solution)/shard_map/all_gather | solution.py:20
  99.7 9.9 %fusion.11 = (f32[1024]{0:T(1024)S(1)}, f32[1024,1024]{0,1:T(8,128)}) fusion(bf16[1024,2048]{1,0:T(8,128)(2,1)} %all-gather.2.cloned.1.call-done, bf16[1024,2048]{1,0:T(8,128)(2,1)} %param.6), kind=kOutput, calls=%fused_computation.36 | convolution fusion | flops 4296014848 | bytes 12587008 | tf_op jit(solution)/shard_map/dot_general | solution.py:23
  109.6 58.9 %pmax.7 = f32[1024]{0:T(1024)S(1)} all-reduce(f32[1024]{0:T(1024)S(1)} %get-tuple-element.14), channel_id=1, replica_groups=mesh['seq'=8,'vocab'=32] {'vocab'}, use_global_device_ids=true, to_apply=%region_3.4 | all-reduce | flops 1024 | bytes 8192 | tf_op jit(solution)/shard_map/pmax | solution.py:30
  168.5 3.3 select_reduce_fusion
  171.8 66.0 %all-reduce.1 = (f32[1024]{0:T(1024)S(1)}, f32[1024]{0:T(1024)S(1)}) all-reduce(f32[1024]{0:T(1024)S(1)} %get-tuple-element.4, f32[1024]{0:T(1024)S(1)} %get-tuple-element.3), channel_id=1, replica_groups=mesh['seq'=8,'vocab'=32] {'vocab'}, use_global_device_ids=true, to_apply=%region_5.6 | all-reduce | flops 2048 | bytes 16384 | tf_op jit(solution)/shard_map/psum | solution.py:32
  237.8 10.2 %convolution_convert_fusion.1 = bf16[1024,2048]{1,0:T(8,128)(2,1)} fusion(bf16[1024,2048]{1,0:T(8,128)(2,1)} %param.6, f32[1024,1024]{0,1:T(8,128)} %get-tuple-element.15, f32[1024]{0:T(1024)S(1)} %get-tuple-element.8, s32[1024]{0:T(1024)S(1)} %broadcast_subtract_fusion, pred[1024]{0:T(1024)(128)(4,1)S(1)} %get-tuple-element.9), kind=kOutput, calls=%fused_computation.5 | convolution fusion | flops 4304404480 | bytes 12592128 | tf_op jit(solution)/shard_map/dot_general | solution.py:45
  248.3 10.1 %convolution_convert_fusion = bf16[1024,2048]{1,0:T(8,128)(2,1)} fusion(bf16[1024,2048]{1,0:T(8,128)(2,1)} %all-gather.2.cloned.1.call-done, f32[1024,1024]{0,1:T(8,128)} %get-tuple-element.15, f32[1024]{0:T(1024)S(1)} %get-tuple-element.8, s32[1024]{0:T(1024)S(1)} %broadcast_subtract_fusion, pred[1024]{0:T(1024)(128)(4,1)S(1)} %get-tuple-element.9), kind=kOutput, calls=%fused_computation.4 | convolution fusion | flops 4304404480 | bytes 12592128 | tf_op jit(solution)/shard_map/dot_general | solution.py:50
  258.3 0.6 copy-done
  259.0 0.7 compare_convert_fusion
  259.6 5.2 %all-to-all-start = ((f32[8,1,4]{2,1,0:T(1,128)}), f32[8,1,4]{2,1,0:T(1,128)S(1)}, u32[]{:S(2)}, u32[]{:S(2)}) async-start(f32[8,1,4]{2,1,0:T(1,128)} %compare_convert_fusion), calls=%async_computation | async-start | bytes 8192 | tf_op jit(solution)/shard_map/all_to_all | solution.py:104
  265.2 1.2 compare_select_fusion.1
  266.6 4.4 all-to-all-done
  271.6 0.7 all_to_all.11
  272.2 3.2 all-to-all-start.1
  275.5 6.1 %all-to-all-done.1 = f32[8,1,4]{2,1,0:T(1,128)S(1)} async-done(((f32[8,1,4]{2,1,0:T(1,128)}), f32[8,1,4]{2,1,0:T(1,128)S(1)}, u32[]{:S(2)}, u32[]{:S(2)}) %all-to-all-start.1) | async-done | bytes 160 | tf_op jit(solution)/shard_map/all_to_all | solution.py:97
  282.1 0.7 reduce.10
  282.8 0.6 convolution_bitcast_fusion
  283.5 97.7 %reduce-scatter.3.cloned.1.call-done = bf16[32,2048]{1,0:T(8,128)(2,1)} async-done(((bf16[1024,2048]{1,0:T(8,128)(2,1)}), bf16[32,2048]{1,0:T(8,128)(2,1)}) %reduce-scatter.3.cloned.1.call-update) | async-done | bytes 131088 | tf_op jit(solution)/shard_map/reduce_scatter | solution.py:44
  381.2 57.7 %reduce-scatter.5.cloned.1.call-done = bf16[1024,256]{1,0:T(8,128)(2,1)} async-done(((bf16[1024,2048]{1,0:T(8,128)(2,1)}), bf16[1024,256]{1,0:T(8,128)(2,1)}) %reduce-scatter.5.cloned.1.call-update) | async-done | bytes 524304 | tf_op jit(solution)/shard_map/reduce_scatter | solution.py:53
  (26 shorter events, 2.1 us)
Async XLA Ops:
  7.2 92.5 %all-gather.2.cloned.1.call-start = ((), (), s32[]{:S(2)}) async-start(), calls=%async_computation.4 | async-start | bytes 4325376 | tf_op jit(solution)/shard_map/all_gather | solution.py:20
  7.9 373.3 %reduce-scatter.3.cloned.1.call-start = ((), (), s32[]{:S(2)}) async-start(), calls=%async_computation.5 | async-start | bytes 4325376 | tf_op jit(solution)/shard_map/reduce_scatter | solution.py:44
  248.0 190.9 %reduce-scatter.5.cloned.1.call-start = ((), (), s32[]{:S(2)}) async-start(), calls=%async_computation.6 | async-start | bytes 4718592 | tf_op jit(solution)/shard_map/reduce_scatter | solution.py:53
  258.3 0.7 copy-start
  259.6 11.3 %all-to-all-start = ((f32[8,1,4]{2,1,0:T(1,128)}), f32[8,1,4]{2,1,0:T(1,128)S(1)}, u32[]{:S(2)}, u32[]{:S(2)}) async-start(f32[8,1,4]{2,1,0:T(1,128)} %compare_convert_fusion), calls=%async_computation | async-start | bytes 8192 | tf_op jit(solution)/shard_map/all_to_all | solution.py:104
  272.2 9.3 %all-to-all-start.1 = ((f32[8,1,4]{2,1,0:T(1,128)}), f32[8,1,4]{2,1,0:T(1,128)S(1)}, u32[]{:S(2)}, u32[]{:S(2)}) async-start(f32[8,1,4]{2,1,0:T(1,128)} %bitcast.9), calls=%async_computation.1 | async-start | bytes 8192 | tf_op jit(solution)/shard_map/all_to_all | solution.py:97
Sparse Core Ops, SparseCore 0:
  10.8 88.8 all-gather.1
  248.1 132.9 reduce-scatter.2
  384.5 54.3 reduce-scatter.4
where the time goes:
time: 447 us; the launch traced here: 445 us
  waiting for transfers between devices  233 us (52%)
  blocking collectives  145 us (32%)
  matrix products  31.1 us (7%)
  between operations  15.7 us (4%)
  starting transfers between devices  8.71 us (2%)
  other arithmetic  6.53 us (1%)
  local copies, waits for them, and re-layouts  5.58 us (1%)
    reduce_scatter x1, waiting for transfers between devices, head_step(): lax.psum_scatter(jnp.dot(logit_grads, weight, preferred_element_type=jnp....  97.7 us
    all_gather x1, waiting for transfers between devices, head_step(): lax.all_gather(block_rows, 'vocab', axis=0, tiled=True)  66.2 us
    psum x1, blocking collectives, head_step(): row_total, target_logit = lax.psum((local_total, target_part), 'vocab')  66 us
    pmax x1, blocking collectives, head_step(): row_top = lax.pmax(local_top, 'vocab')  58.9 us
    reduce_scatter x1, waiting for transfers between devices, head_step(): lax.psum_scatter(partial_value.astype(jnp.bfloat16), 'seq', scatter_dimen...  57.7 us
    unnamed x1, blocking collectives  20.2 us
    dot_general x1, matrix products, head_step(): jnp.dot(logit_grads, weight, preferred_element_type=jnp.float32)  10.2 us
    dot_general x1, matrix products, head_step(): lax.dot_general(logit_grads, all_rows, (((0,), (0,)), ((), ())), preferre...  10.1 us
  transfers between devices with their start and end apart: 5, of which 5 were waited for; matrix products, arithmetic and copies ran while one was open for 4% of the time, Pallas kernels for 0%

commit v1 on v0

v1 whole, which is shorter than its diff:
```python
import itertools

import jax
import jax.numpy as jnp
from jax import lax
from jax.experimental import pallas as pl
from jax.experimental.pallas import tpu as pltpu
from jax.sharding import PartitionSpec as P

LOSS_SCALE = 4.0
D = 2048
VD = 1024
RD = 16
NV = 32
R = RD * NV
NS = 8
CW = D // NS
HX = D + 128
Y_CHUNKS = [(112 * k, 112) for k in range(4)]
X_CHUNKS = [(448 + 144 * k, 144) for k in range(4)]
F32, BF16 = jnp.float32, jnp.bfloat16
MESH = pl.DeviceIdType.MESH


def nt(a, b):
    return lax.dot_general(a, b, (((1,), (1,)), ((), ())), preferred_element_type=F32)


def nn(a, b):
    return jnp.dot(a, b, preferred_element_type=F32)


def body(
    spans, counts, targets, hidden, weight,
    code_out, hid_out, loss_out,
    w, hx, lg, gt, g,
    st_mine, st_in, tot_mine, tot_in, loss_mine, loss_in,
    cp, y_in, xa_in, xl_in, xr_in, xx_a, xx_l, xx_r, yy_in, xs, xxs,
    hd_out, hd_in, hacc, za_out, za_in, zl_in, zr_in, zh_out, zh_in,
    ssem, rsem, wsem,
):
    me_s, me_v = lax.axis_index("seq"), lax.axis_index("vocab")
    x, y = lax.rem(me_s, 4), me_s // 4
    z, h, c = me_v // 4, lax.rem(me_v // 2, 2), lax.rem(me_v, 2)
    ids = itertools.count()
    sent = []

    def at(xx=None, yy=None, zz=None, hh=None, cc=None):
        xx, yy, zz, hh, cc = (
            mine if other is None else other
            for other, mine in ((xx, x), (yy, y), (zz, z), (hh, h), (cc, c))
        )
        return {"seq": yy * 4 + xx, "vocab": zz * 4 + hh * 2 + cc}

    def send(src, dst, device):
        i = next(ids)
        copy = pltpu.make_async_remote_copy(
            src_ref=src, dst_ref=dst, send_sem=ssem.at[i], recv_sem=rsem.at[i],
            device_id=device, device_id_type=MESH,
        )
        copy.start()
        sent.append(copy)
        return i, device

    def arrive(ticket, where):
        i, device = ticket
        pltpu.make_async_remote_copy(
            src_ref=where, dst_ref=where, send_sem=ssem.at[i], recv_sem=rsem.at[i],
            device_id=device, device_id_type=MESH,
        ).wait_recv()

    right_x, left_x, far_x = (lax.rem(x + k, 4) for k in (1, 3, 2))
    zs = [lax.rem(z + k, 8) for k in range(8)]
    other_c, other_h, other_y = at(cc=1 - c), at(hh=1 - h), at(yy=1 - y)
    layer = [other_c, other_h, at(hh=1 - h, cc=1 - c)]
    column = [at(zz=zs[k]) for k in range(1, 8)]
    others = [
        {"seq": lax.rem(me_s + k, NS), "vocab": me_v} for k in range(1, NS)
    ]

    weight_in = pltpu.make_async_copy(weight, w, wsem)
    weight_in.start()
    barrier = pltpu.get_barrier_semaphore()
    for device in layer + column + others:
        pl.semaphore_signal(barrier, inc=1, device_id=device, device_id_type=MESH)

    s0 = spans[0, 0, 0]

    def position(shape):
        rank = lax.broadcasted_iota(jnp.int32, shape, 0)
        return jnp.where(rank < s0, RD - s0 + rank, RD + rank)

    pick = (position((RD, 2 * RD)) == lax.broadcasted_iota(jnp.int32, (RD, 2 * RD), 1)).astype(F32).astype(BF16)
    packed = nn(pick, hidden[0, 0].reshape(2 * RD, D)).astype(BF16)
    place = position((RD, 128))
    code = jnp.zeros((RD, 128), jnp.int32)
    for q in range(2):
        for p in range(RD):
            code = jnp.where(place == q * RD + p, targets[0, 0, q, p], code)
    lane = lax.broadcasted_iota(jnp.int32, (RD, 128), 1)
    extra = jnp.where(lane == 0, code // 256, jnp.where(lane == 1, lax.rem(code, 256), 0))

    def rows(zz, hh, cc):
        return pl.ds(pl.multiple_of(cc * 256 + zz * 32 + hh * 16, 16), 16)

    def block(zz, hh, cc=c):
        return hx.at[rows(zz, hh, cc)]

    mine = block(z, h)
    hx[rows(z, h, c), 0:D] = packed
    hx[rows(z, h, c), D:HX] = extra.astype(F32).astype(BF16)
    pl.semaphore_wait(barrier, len(layer + column + others))

    up, down = at(zz=zs[1]), at(zz=zs[7])
    hs = (h, 1 - h)
    from_y = send(mine, mine, other_h)
    ups, downs = [None, None], [None, None]
    crossed = []

    def cross(zz, hh):
        crossed.append((send(block(zz, hh), block(zz, hh), other_c), zz, hh))

    ups[0], downs[0] = send(mine, mine, up), send(mine, mine, down)
    cross(z, h)
    arrive(from_y, block(z, 1 - h))
    other = block(z, 1 - h)
    ups[1], downs[1] = send(other, other, up), send(other, other, down)
    cross(z, 1 - h)
    for k in range(1, 5):
        below, above = zs[8 - k], zs[k]
        next_ups, next_downs = [None, None], [None, None]
        for b in range(2):
            if ups[b] is not None:
                here = block(below, hs[b])
                arrive(ups[b], here)
                if k < 3 or (k == 3 and b == 0):
                    next_ups[b] = send(here, here, up)
                cross(below, hs[b])
            if downs[b] is not None:
                here = block(above, hs[b])
                arrive(downs[b], here)
                if k < 3 or (k == 3 and b == 1):
                    next_downs[b] = send(here, here, down)
                cross(above, hs[b])
        ups, downs = next_ups, next_downs
    for ticket, zz, hh in crossed:
        arrive(ticket, block(zz, hh, 1 - c))
    weight_in.wait()

    def logits_of(k, _):
        at_k = pl.ds(pl.multiple_of(k * 256, 256), 256)
        lg[at_k, :] = nt(w[at_k, :], hx[:, 0:D])
        return 0

    lax.fori_loop(0, VD // 256, logits_of, 0)

    ones = lax.broadcasted_iota(jnp.int32, (8, 128), 0) == lax.broadcasted_iota(jnp.int32, (8, 128), 1)
    halves = nt(ones.astype(F32).astype(BF16), hx[:, D:HX])
    marked = (halves[0:1] * 256.0 + halves[1:2]).astype(jnp.int32) - me_v * VD
    top = jnp.max(lg[...], axis=0, keepdims=True)

    def sums_of(k, carry):
        total, named = carry
        at_k = pl.ds(pl.multiple_of(k * 64, 64), 64)
        part = lg[at_k, :]
        code_at = lax.broadcasted_iota(jnp.int32, (64, R), 0) + k * 64
        named = named + jnp.sum(jnp.where(code_at == marked, part, 0.0), axis=0, keepdims=True)
        grown = jnp.exp(part - top)
        lg[at_k, :] = grown
        return total + jnp.sum(grown, axis=0, keepdims=True), named

    total, named = lax.fori_loop(
        0, VD // 64, sums_of, (jnp.zeros((1, R), F32), jnp.zeros((1, R), F32))
    )

    def fold(row):
        return [row[:, 128 * k : 128 * (k + 1)] for k in range(R // 128)]

    def join(tops, totals, nameds):
        best = tops[0]
        for other_top in tops[1:]:
            best = jnp.maximum(best, other_top)
        total = sum(t * jnp.exp(m - best) for t, m in zip(totals, tops))
        return best, total, sum(nameds)

    def exchange(triple, out_ref, in_ref, devices):
        out_ref[0:4], out_ref[4:8], out_ref[8:12] = triple
        out_ref[12:16] = jnp.zeros((4, 128), F32)
        tickets = [send(out_ref, in_ref.at[k], device) for k, device in enumerate(devices)]
        for k, ticket in enumerate(tickets):
            arrive(ticket, in_ref.at[k])
        parts = [triple] + [
            (in_ref[k, 0:4], in_ref[k, 4:8], in_ref[k, 8:12]) for k in range(len(devices))
        ]
        return join(*zip(*parts))

    triple = tuple(jnp.concatenate(fold(row), axis=0) for row in (top, total, named))
    triple = exchange(triple, st_mine, st_in, layer)
    row_top, row_total, row_named = exchange(triple, tot_mine, tot_in, column)
    log_total = row_top + jnp.log(row_total)
    loss_mine[0:4] = log_total - row_named
    lanes8 = lax.broadcasted_iota(jnp.int32, (4, 128), 1)
    sends = jnp.zeros((4, 128), F32)
    for j in range(NS):
        sends = jnp.where(lanes8 == j, counts[0, 0, j].astype(F32), sends)
    loss_mine[4:8] = sends
    loss_tickets = [send(loss_mine, loss_in.at[k], device) for k, device in enumerate(others)]

    factor = LOSS_SCALE * jnp.exp(
        top - jnp.concatenate([log_total[k : k + 1] for k in range(R // 128)], axis=1)
    )

    def grads_of(start, size):
        code_at = lax.broadcasted_iota(jnp.int32, (size, R), 0) + start
        grad = lg[start : start + size, :] * factor - jnp.where(code_at == marked, LOSS_SCALE, 0.0)
        gt[start : start + size, :] = grad.astype(BF16)

    def part(chunk, s):
        start, size = chunk
        return nn(gt[start : start + size, :], hx[:, pl.ds(pl.multiple_of(s * CW, CW), CW)])

    y_tickets = []
    for k, chunk in enumerate(Y_CHUNKS):
        start, size = chunk
        grads_of(start, size)
        for xx in range(4):
            cp[xx, start : start + size, :] = part(chunk, (1 - y) * 4 + xx).astype(BF16)
        y_tickets.append(send(cp.at[:, start : start + size], y_in.at[:, start : start + size], other_y))
    first_x = X_CHUNKS[0][0]
    a_tickets = []
    for k, chunk in enumerate(X_CHUNKS):
        start, size = chunk
        grads_of(start, size)
        spot = slice(start - first_x, start - first_x + size)
        pair = []
        for q, device in enumerate((at(xx=right_x), at(xx=left_x))):
            xxs[q, spot, :] = part(chunk, q * 4 + far_x).astype(BF16)
            pair.append(send(xxs.at[q, spot], xx_a.at[q, spot], device))
        a_tickets.append(pair)

    def turn(k, _):
        at_k = pl.ds(pl.multiple_of(k * 256, 256), 256)
        g[:, at_k] = gt[at_k, :].astype(F32).T.astype(BF16)
        return 0

    lax.fori_loop(0, VD // 256, turn, 0)

    def core_rows(cc):
        return pl.ds(pl.multiple_of(cc * 256, 256), 256)

    def theirs(k, _):
        at_k = pl.ds(pl.multiple_of(k * 512, 512), 512)
        hd_out[:, at_k] = nn(g[core_rows(1 - c), :], w[:, at_k]).astype(BF16)
        return 0

    lax.fori_loop(0, D // 512, theirs, 0)
    d_ticket = send(hd_out, hd_in, other_c)

    lr_tickets = []
    for k, chunk in enumerate(X_CHUNKS):
        start, size = chunk
        spot = slice(start - first_x, start - first_x + size)
        pair = []
        for side, (to, into) in enumerate(((right_x, xx_l), (left_x, xx_r))):
            arrive(a_tickets[k][side], xx_a.at[side, spot])
            for q in range(2):
                value = part(chunk, q * 4 + to)
                if q == side:
                    value = value + xx_a[q, spot, :].astype(F32)
                xxs[2 + 2 * side + q, spot, :] = value.astype(BF16)
            pair.append(
                send(xxs.at[2 + 2 * side : 4 + 2 * side, spot], into.at[:, spot], at(xx=to))
            )
        lr_tickets.append(pair)

    arrive(d_ticket, hd_in)

    def ours(k, _):
        at_k = pl.ds(pl.multiple_of(k * 512, 512), 512)
        hacc[:, at_k] = nn(g[core_rows(c), :], w[:, at_k]) + hd_in[:, at_k].astype(F32)
        return 0

    lax.fori_loop(0, D // 512, ours, 0)

    def layer_rows(zz, first=0, size=32):
        return pl.ds(pl.multiple_of(zz * 32 + first, 16), size)

    za_out[0] = hacc[layer_rows(zs[4], 0, 16), :].astype(BF16)
    za_out[1] = hacc[layer_rows(zs[4], 16, 16), :].astype(BF16)
    z_up = send(za_out.at[0], za_in.at[0], up)
    z_down = send(za_out.at[1], za_in.at[1], down)

    def z_step(k, z_up, z_down):
        outs = []
        for side, (ticket, into, to, owner) in enumerate(
            ((z_up, zl_in, up, zs[4 - k]), (z_down, zr_in, down, zs[4 + k]))
        ):
            own = hacc[layer_rows(owner), :]
            if k == 1:
                arrive(ticket, za_in.at[side])
                other = za_in[side].astype(F32)
                if side == 0:
                    value = jnp.concatenate([own[0:16] + other, own[16:32]], axis=0)
                else:
                    value = jnp.concatenate([own[0:16], own[16:32] + other], axis=0)
            else:
                arrive(ticket, into.at[k - 2])
                value = own + into[k - 2].astype(F32)
            zh_out[side, k - 1] = value.astype(BF16)
            outs.append(send(zh_out.at[side, k - 1], into.at[k - 1], to))
        return outs

    yy_tickets = []
    for k, chunk in enumerate(X_CHUNKS):
        start, size = chunk
        spot = slice(start - first_x, start - first_x + size)
        arrive(lr_tickets[k][0], xx_l.at[:, spot])
        arrive(lr_tickets[k][1], xx_r.at[:, spot])
        value = part(chunk, (1 - y) * 4 + x)
        value = value + xx_l[1 - y, spot, :].astype(F32) + xx_r[1 - y, spot, :].astype(F32)
        xxs[6, spot, :] = value.astype(BF16)
        yy_tickets.append(send(xxs.at[6, spot], yy_in.at[spot], other_y))
        if k == 1:
            z_up, z_down = z_step(1, z_up, z_down)

    def y_arrived(chunk, xx):
        start, size = chunk
        return part(chunk, y * 4 + xx) + y_in[xx, start : start + size, :].astype(F32)

    xa_tickets, xlr_tickets = {}, {}

    def first_hop(k):
        start, size = Y_CHUNKS[k]
        half = size // 32 * 16
        arrive(y_tickets[k], y_in.at[:, start : start + size])
        xs[0, start : start + size, :] = y_arrived(Y_CHUNKS[k], far_x).astype(BF16)
        pair = []
        for spot, device in (
            (slice(start, start + half), at(xx=right_x)),
            (slice(start + half, start + size), at(xx=left_x)),
        ):
            pair.append((send(xs.at[0, spot], xa_in.at[spot], device), spot))
        xa_tickets[k] = pair

    def second_hop(k):
        start, size = Y_CHUNKS[k]
        half = size // 32 * 16
        all_rows = slice(start, start + size)
        pair = []
        for side, (to, into) in enumerate(((right_x, xl_in), (left_x, xr_in))):
            ticket, spot = xa_tickets[k][side]
            arrive(ticket, xa_in.at[spot])
            value = y_arrived(Y_CHUNKS[k], to)
            other = xa_in[spot, :].astype(F32)
            if side == 0:
                value = jnp.concatenate([value[:half] + other, value[half:]], axis=0)
            else:
                value = jnp.concatenate([value[:half], value[half:] + other], axis=0)
            xs[1 + side, all_rows, :] = value.astype(BF16)
            pair.append(send(xs.at[1 + side, all_rows], into.at[all_rows], at(xx=to)))
        xlr_tickets[k] = pair

    def y_finish(k):
        start, size = Y_CHUNKS[k]
        spot = slice(start, start + size)
        arrive(xlr_tickets[k][0], xl_in.at[spot])
        arrive(xlr_tickets[k][1], xr_in.at[spot])
        value = y_arrived(Y_CHUNKS[k], x)
        value = value + xl_in[spot, :].astype(F32) + xr_in[spot, :].astype(F32)
        code_out[spot, :] = value.astype(BF16)

    n = len(Y_CHUNKS)
    for k in range(n + 2):
        if k < n:
            first_hop(k)
        if k < 2:
            z_up, z_down = z_step(k + 2, z_up, z_down)
        if 0 <= k - 1 < n:
            second_hop(k - 1)
        if k == 2:
            arrive(z_up, zl_in.at[2])
            arrive(z_down, zr_in.at[2])
            summed = hacc[layer_rows(z), :] + zl_in[2].astype(F32) + zr_in[2].astype(F32)
            zh_in[1:3] = summed.reshape(2, RD, D)
            zh_out[0, 3, 0:16] = zh_in[1 + (1 - h)].astype(BF16)
            h_ticket = send(zh_out.at[0, 3, 0:16], za_in.at[2], other_h)
        if 0 <= k - 2 < n:
            y_finish(k - 2)

    for k, chunk in enumerate(X_CHUNKS):
        start, size = chunk
        spot = slice(start - first_x, start - first_x + size)
        arrive(yy_tickets[k], yy_in.at[spot])
        value = part(chunk, y * 4 + x) + yy_in[spot, :].astype(F32)
        value = value + xx_l[y, spot, :].astype(F32) + xx_r[y, spot, :].astype(F32)
        code_out[start : start + size, :] = value.astype(BF16)

    arrive(h_ticket, za_in.at[2])
    own = (zh_in[1 + h] + za_in[2].astype(F32)).astype(BF16)
    spread = (
        position_row(s0) == lax.broadcasted_iota(jnp.int32, (2 * RD, RD), 0)
    ).astype(F32).astype(BF16)
    hid_out[...] = nn(spread, own).astype(BF16)

    tiles = [loss_mine[...]]
    for k, ticket in enumerate(loss_tickets):
        arrive(ticket, loss_in.at[k])
        tiles.append(loss_in[k])
    lane1 = lax.broadcasted_iota(jnp.int32, (1, 128), 1)
    own_row = lax.broadcasted_iota(jnp.int32, (4, 128), 0) == (c * 2 + z // 4)
    rank = lane1 - (lax.rem(z, 4) * 32 + h * 16)
    in_block = (rank >= 0) & (rank < RD)
    slots = lax.broadcasted_iota(jnp.int32, (RD, 128), 0)
    got, before, losses = [], [], []
    for tile in tiles:
        row = tile[4:5]
        got.append(jnp.sum(jnp.where(lane1 == me_s, row, 0.0), axis=1, keepdims=True).astype(jnp.int32))
        before.append(jnp.sum(jnp.where(lane1 < me_s, row, 0.0), axis=1, keepdims=True).astype(jnp.int32))
        losses.append(jnp.sum(jnp.where(own_row, tile[0:4], 0.0), axis=0, keepdims=True))
    listed = jnp.zeros((RD, 128), F32)
    for k in range(NS):
        source = lax.rem(me_s + NS - k, NS)
        first = jnp.zeros((1, 1), jnp.int32)
        for j in range(NS):
            earlier = lax.rem(me_s + NS - j, NS) < source
            first = first + jnp.where(earlier, got[j], 0)
        offset = rank - before[k]
        live = in_block & (offset >= 0) & (offset < got[k])
        slot = jnp.where(live, first + offset, -1)
        listed = listed + jnp.where(slots == slot, losses[k], 0.0)
    loss_out[...] = listed

    for copy in sent:
        copy.wait_send()


def position_row(s0):
    rank = lax.broadcasted_iota(jnp.int32, (2 * RD, RD), 1)
    return jnp.where(rank < s0, RD - s0 + rank, RD + rank)


def per_device(hidden, head_weight, targets, span_counts, send_counts):
    ny = Y_CHUNKS[-1][0] + Y_CHUNKS[-1][1]
    nx = VD - ny
    vmem, smem = pl.BlockSpec(memory_space=pltpu.VMEM), pl.BlockSpec(memory_space=pltpu.SMEM)
    copies = 256
    code_grad, hidden_grad, listed = pl.pallas_call(
        body,
        out_shape=(
            jax.ShapeDtypeStruct((VD, CW), BF16),
            jax.ShapeDtypeStruct((2 * RD, D), BF16),
            jax.ShapeDtypeStruct((RD, 128), F32),
        ),
        in_specs=[smem, smem, smem, vmem, pl.BlockSpec(memory_space=pl.ANY)],
        out_specs=(vmem, vmem, vmem),
        scratch_shapes=[
            pltpu.VMEM((VD, D), BF16),
            pltpu.VMEM((R, HX), BF16),
            pltpu.VMEM((VD, R), F32),
            pltpu.VMEM((VD, R), BF16),
            pltpu.VMEM((R, VD), BF16),
            pltpu.VMEM((16, 128), F32),
            pltpu.VMEM((3, 16, 128), F32),
            pltpu.VMEM((16, 128), F32),
            pltpu.VMEM((7, 16, 128), F32),
            pltpu.VMEM((8, 128), F32),
            pltpu.VMEM((7, 8, 128), F32),
            pltpu.VMEM((4, ny, CW), BF16),
            pltpu.VMEM((4, ny, CW), BF16),
            pltpu.VMEM((ny, CW), BF16),
            pltpu.VMEM((ny, CW), BF16),
            pltpu.VMEM((ny, CW), BF16),
            pltpu.VMEM((2, nx, CW), BF16),
            pltpu.VMEM((2, nx, CW), BF16),
            pltpu.VMEM((2, nx, CW), BF16),
            pltpu.VMEM((nx, CW), BF16),
            pltpu.VMEM((3, ny, CW), BF16),
            pltpu.VMEM((7, nx, CW), BF16),
            pltpu.VMEM((256, D), BF16),
            pltpu.VMEM((256, D), BF16),
            pltpu.VMEM((256, D), F32),
            pltpu.VMEM((2, 16, D), BF16),
            pltpu.VMEM((3, 16, D), BF16),
            pltpu.VMEM((3, 32, D), BF16),
            pltpu.VMEM((3, 32, D), BF16),
            pltpu.VMEM((2, 4, 32, D), BF16),
            pltpu.VMEM((3, 16, D), F32),
            pltpu.SemaphoreType.DMA((copies,)),
            pltpu.SemaphoreType.DMA((copies,)),
            pltpu.SemaphoreType.DMA,
        ],
        compiler_params=pltpu.CompilerParams(
            collective_id=0, has_side_effects=True, vmem_limit_bytes=56 * 1024 * 1024
        ),
        name="head",
    )(span_counts, send_counts, targets, hidden, head_weight)
    return (
        jnp.sum(listed, axis=1).reshape(1, 1, RD),
        hidden_grad.reshape(hidden.shape),
        code_grad,
    )


def solution(mesh):
    in_specs = (
        P("seq", "vocab", None, None, None),
        P("vocab", None),
        P("seq", "vocab", None, None),
        P("seq", "vocab", None),
        P("seq", "vocab", None),
    )
    out_specs = (P("seq", "vocab", None), P("seq", "vocab", None, None, None), P("vocab", "seq"))
    return jax.shard_map(
        per_device, mesh=mesh, in_specs=in_specs, out_specs=out_specs, check_vma=False
    )
```

time: 447 us -> 93.7 us (0.21)
  waiting for transfers between devices: 233 us -> 0 us
  blocking collectives: 145 us -> 0 us
  Pallas kernels: 0 us -> 87.1 us
  matrix products: 31.1 us -> 0 us
  between operations: 15.7 us -> 0.64 us
  starting transfers between devices: 8.71 us -> 0 us
  other arithmetic: 6.53 us -> 1.32 us
    reduce_scatter x2 -> x0, waiting for transfers between devices: 155 us -> none  [the longest x1 97.7 us: head_step(): lax.psum_scatter(jnp.dot(logit_grads, weight, preferred_element_type=jnp....]
    pallas_call x0 -> x1, Pallas kernels: none -> 87.1 us  [per_device(): pl.pallas_call(body, out_shape=(jax.ShapeDtypeStruct((VD, CW), BF16), jax...]
    all_gather x1 -> x0, waiting for transfers between devices: 66.2 us -> none  [head_step(): lax.all_gather(block_rows, 'vocab', axis=0, tiled=True)]
    psum x1 -> x0, blocking collectives: 66 us -> none  [head_step(): row_total, target_logit = lax.psum((local_total, target_part), 'vocab')]
    pmax x1 -> x0, blocking collectives: 58.9 us -> none  [head_step(): row_top = lax.pmax(local_top, 'vocab')]
    dot_general x5 -> x0, matrix products: 31.1 us -> none  [the longest x1 10.2 us: head_step(): jnp.dot(logit_grads, weight, preferred_element_type=jnp.float32)]
    unnamed x1 -> x0, blocking collectives: 20.2 us -> none
    all_to_all x2 -> x0, waiting for transfers between devices: 10.5 us -> none  [the longest x1 6.07 us: per_device(): lax.all_to_all(slot_loss.reshape(partner_device_count, count_of_slots), '...]
  transfers between devices with their start and end apart: 5 -> 0, of which waited for: 5 -> 0; matrix products, arithmetic and copies ran while one was open for 4% -> 0% of each run, Pallas kernels for 0% -> 0%
where the time goes in v1:
time: 93.7 us; the launch traced here: 92.5 us
  Pallas kernels  87.1 us (93%)
  local copies, waits for them, and re-layouts  3.43 us (4%)
  other arithmetic  1.32 us (1%)
    pallas_call x1, Pallas kernels, per_device(): pl.pallas_call(body, out_shape=(jax.ShapeDtypeStruct((VD, CW), BF16), jax...  87.1 us
    unnamed x2, local copies, waits for them, and re-layouts  3.43 us

profile of v1, /device:TPU:32, one launch (start us, length us, event | category | flops | bytes accessed | tf_op | source)
XLA Modules:
  0.0 92.5 jit_solution(17059834769340046784)
XLA Ops:
  0.6 87.1 %head.1 = (bf16[1024,256]{1,0:T(8,128)(2,1)}, bf16[32,2048]{1,0:T(8,128)(2,1)}, f32[16,128]{1,0:T(8,128)}) custom-call(s32[1,1,2]{2,1,0:T(1,128)} %spans.1, s32[1,1,8]{2,1,0:T(1,128)} %counts.1, s32[1,1,2,16]{3,2,1,0:T(2,128)} %targets.1, bf16[1,1,2,16,2048]{4,3,2,1,0:T(8,128)(2,1)} %hidden.1, bf16[1024,2048]{1,0:T(8,128)(2,1)} %weight.1), custom_call_target="tpu_custom_call" | custom-call | tf_op jit(solution)/shard_map/head/pallas_call | solution.py:447
  87.7 1.3 %reduce_sum.9 = f32[16]{0:T(128)} reduce(f32[16,128]{1,0:T(8,128)} %get-tuple-element.6, f32[]{:T(128)} %constant.0.clone.1), dimensions={1}, to_apply=%region_0.0 | reduce | flops 2032 | bytes 8260 | tf_op jit(solution)/shard_map/reduce_sum | solution.py:498
  89.0 1.6 %copy.10 = bf16[1,1,2,16,2048]{4,3,2,1,0:T(8,128)(2,1)} copy(bf16[1,1,2,16,2048]{4,3,2,1,0:T(8,128)(2,1)} %bitcast.2) | data formatting | bytes 262144
  90.6 1.9 %copy.11 = bf16[1024,256]{1,0:T(8,128)(2,1)} copy(bf16[1024,256]{1,0:T(8,128)(2,1)} %get-tuple-element.14) | data formatting | bytes 1048576

commit v2 on v1

v2 whole, which is shorter than its diff:
```python
import itertools

import jax
import jax.numpy as jnp
from jax import lax
from jax.experimental import pallas as pl
from jax.experimental.pallas import tpu as pltpu
from jax.sharding import PartitionSpec as P

LOSS_SCALE = 4.0
D = 2048
VD = 1024
RD = 16
NV = 32
R = RD * NV
NS = 8
CW = D // NS
HX = D + 128
CHUNKS = [(256 * k, 256) for k in range(4)]
FAR = (4, 3, 5, 2, 6, 1, 7, 0)
GROUPS = ((0, 1), (1, 3), (3, 5), (5, 8))
F32, BF16 = jnp.float32, jnp.bfloat16
MESH = pl.DeviceIdType.MESH


def nt(a, b):
    return lax.dot_general(a, b, (((1,), (1,)), ((), ())), preferred_element_type=F32)


def nn(a, b):
    return jnp.dot(a, b, preferred_element_type=F32)


def body(
    spans, counts, targets, hidden, weight,
    code_out, hid_out, loss_out,
    w, hx, lg, gt, g,
    st_mine, st_in, tot_mine, tot_in, lt_mine, lt_in, loss_mine, loss_in,
    xs, xa_in, xl_in, xr_in,
    hd_out, hd_in, hacc, yo, yi, zo, zi,
    ssem, rsem, wsem,
):
    me_s, me_v = lax.axis_index("seq"), lax.axis_index("vocab")
    x, y = lax.rem(me_s, 4), me_s // 4
    z, h, c = me_v // 4, lax.rem(me_v // 2, 2), lax.rem(me_v, 2)
    ids = itertools.count()
    sent = []

    def at(xx=None, yy=None, zz=None, hh=None, cc=None):
        xx, yy, zz, hh, cc = (
            mine if other is None else other
            for other, mine in ((xx, x), (yy, y), (zz, z), (hh, h), (cc, c))
        )
        return {"seq": yy * 4 + xx, "vocab": zz * 4 + hh * 2 + cc}

    def send(src, dst, device):
        i = next(ids)
        copy = pltpu.make_async_remote_copy(
            src_ref=src, dst_ref=dst, send_sem=ssem.at[i], recv_sem=rsem.at[i],
            device_id=device, device_id_type=MESH,
        )
        copy.start()
        sent.append(copy)
        return i, device

    def arrive(ticket, where):
        i, device = ticket
        pltpu.make_async_remote_copy(
            src_ref=where, dst_ref=where, send_sem=ssem.at[i], recv_sem=rsem.at[i],
            device_id=device, device_id_type=MESH,
        ).wait_recv()

    right_x, left_x, far_x = (lax.rem(x + k, 4) for k in (1, 3, 2))
    zs = [lax.rem(z + k, 8) for k in range(8)]
    other_c, other_h = at(cc=1 - c), at(hh=1 - h)
    near_y = [at(yy=1 - y), at(yy=1 - y, hh=1 - h)]
    layer = [other_c, other_h, at(hh=1 - h, cc=1 - c)]
    column = [at(zz=zs[k]) for k in range(1, 8)]
    others = [
        {"seq": lax.rem(me_s + k, NS), "vocab": me_v} for k in range(1, NS)
    ]
    peers = layer + column + others + near_y[1:]

    weight_in = pltpu.make_async_copy(weight, w, wsem)
    weight_in.start()
    barrier = pltpu.get_barrier_semaphore()
    for device in peers:
        pl.semaphore_signal(barrier, inc=1, device_id=device, device_id_type=MESH)

    s0 = spans[0, 0, 0]

    def position(shape, axis):
        rank = lax.broadcasted_iota(jnp.int32, shape, axis)
        return jnp.where(rank < s0, RD - s0 + rank, RD + rank)

    pick = position((RD, 2 * RD), 0) == lax.broadcasted_iota(jnp.int32, (RD, 2 * RD), 1)
    packed = nn(pick.astype(F32).astype(BF16), hidden[0, 0].reshape(2 * RD, D)).astype(BF16)
    place = position((RD, 128), 0)
    code = jnp.zeros((RD, 128), jnp.int32)
    for q in range(2):
        for p in range(RD):
            code = jnp.where(place == q * RD + p, targets[0, 0, q, p], code)
    lane = lax.broadcasted_iota(jnp.int32, (RD, 128), 1)
    extra = jnp.where(lane == 0, code // 256, jnp.where(lane == 1, lax.rem(code, 256), 0))

    def rows(zz, hh, cc, yy, size=16):
        return pl.ds(pl.multiple_of(yy * R + cc * 256 + zz * 32 + hh * 16, 16), size)

    def block(zz, hh, yy=y):
        return hx.at[rows(zz, hh, c, yy)]

    def pair(zz, cc=c, yy=y):
        return hx.at[rows(zz, 0, cc, yy, 32)]

    mine = block(z, h)
    hx[rows(z, h, c, y), 0:D] = packed
    hx[rows(z, h, c, y), D:HX] = extra.astype(F32).astype(BF16)
    pl.semaphore_wait(barrier, len(peers))

    up, down = at(zz=zs[1]), at(zz=zs[7])
    by_z, by_y, by_h = {}, {}, {}
    crossed = {}

    def cross(k, yy=y):
        crossed[k] = send(pair(zs[k], c, yy), pair(zs[k], c, yy), other_c)

    def spread_y(k):
        here = block(zs[k], h)
        by_y[k] = [send(here, here, device) for device in near_y]

    by_h[0] = send(mine, mine, other_h)
    for k in (4, 3, 5, 1, 7, 2, 6):
        by_z[(8 - k) % 8] = send(mine, mine, at(zz=zs[k]))
    spread_y(0)
    arrive(by_h[0], block(z, 1 - h))
    other = block(z, 1 - h)
    ups, downs = send(other, other, up), send(other, other, down)
    cross(0)
    for k in (4, 3, 5):
        here = block(zs[k], h)
        arrive(by_z[k], here)
        by_h[k] = send(here, here, other_h)
        spread_y(k)
    for k in (1, 7):
        arrive(by_z[k], block(zs[k], h))
        spread_y(k)
    here = block(zs[7], 1 - h)
    arrive(ups, here)
    ups = send(here, here, up)
    cross(7)
    here = block(zs[1], 1 - h)
    arrive(downs, here)
    downs = send(here, here, down)
    cross(1)
    for k in (2, 6):
        arrive(by_z[k], block(zs[k], h))
        spread_y(k)
    for k in (4, 3, 5):
        arrive(by_h[k], block(zs[k], 1 - h))
        cross(k)
    arrive(ups, block(zs[6], 1 - h))
    cross(6)
    arrive(downs, block(zs[2], 1 - h))
    cross(2)
    for k in (0, 7, 1, 4, 3, 5, 6, 2):
        arrive(crossed[k], pair(zs[k], 1 - c))
    weight_in.wait()

    own_lanes = pl.ds(pl.multiple_of(y * R, R), R)
    other_lanes = pl.ds(pl.multiple_of((1 - y) * R, R), R)

    def logits_of(k, lanes):
        at_k = slice(256 * k, 256 * (k + 1))
        lg[at_k, lanes] = nt(w[at_k, :], hx[lanes, 0:D])

    own_crossed, crossed = crossed, {}
    for k in range(4):
        logits_of(k, own_lanes)
        for kk in ((0, 4), (3, 5), (1, 7), (2, 6))[k]:
            for device, hh in zip(near_y, (h, 1 - h)):
                ticket = by_y[kk][0 if device is near_y[0] else 1]
                arrive(ticket, block(zs[kk], hh, 1 - y))
            cross(kk, 1 - y)

    ones = lax.broadcasted_iota(jnp.int32, (8, 128), 0) == lax.broadcasted_iota(jnp.int32, (8, 128), 1)
    ones = ones.astype(F32).astype(BF16)

    def marks(lanes):
        halves = nt(ones, hx[lanes, D:HX])
        return (halves[0:1] * 256.0 + halves[1:2]).astype(jnp.int32) - me_v * VD

    marked = marks(own_lanes)
    top = jnp.max(lg[:, own_lanes], axis=0, keepdims=True)

    def sums_of(k, carry):
        total, named = carry
        at_k = pl.ds(pl.multiple_of(k * 64, 64), 64)
        part = lg[at_k, own_lanes]
        code_at = lax.broadcasted_iota(jnp.int32, (64, R), 0) + k * 64
        named = named + jnp.sum(jnp.where(code_at == marked, part, 0.0), axis=0, keepdims=True)
        grown = jnp.exp(part - top)
        lg[at_k, own_lanes] = grown
        return total + jnp.sum(grown, axis=0, keepdims=True), named

    total, named = lax.fori_loop(
        0, VD // 64, sums_of, (jnp.zeros((1, R), F32), jnp.zeros((1, R), F32))
    )

    def fold(row):
        return jnp.concatenate([row[:, 128 * k : 128 * (k + 1)] for k in range(R // 128)], axis=0)

    def unfold(tile):
        return jnp.concatenate([tile[k : k + 1] for k in range(R // 128)], axis=1)

    def join(tops, totals, nameds):
        best = tops[0]
        for other_top in tops[1:]:
            best = jnp.maximum(best, other_top)
        total = sum(t * jnp.exp(m - best) for t, m in zip(totals, tops))
        return best, total, sum(nameds)

    def begin(triple, out_ref, in_ref, devices):
        out_ref[0:4], out_ref[4:8], out_ref[8:12] = triple
        out_ref[12:16] = jnp.zeros((4, 128), F32)
        return [send(out_ref, in_ref.at[k], device) for k, device in enumerate(devices)]

    def end(triple, in_ref, tickets):
        parts = [triple]
        for k, ticket in enumerate(tickets):
            arrive(ticket, in_ref.at[k])
            parts.append((in_ref[k, 0:4], in_ref[k, 4:8], in_ref[k, 8:12]))
        return join(*zip(*parts))

    triple = tuple(fold(row) for row in (top, total, named))
    tickets = begin(triple, st_mine, st_in, layer)
    for k in range(8):
        arrive(crossed[(0, 4, 3, 5, 1, 7, 2, 6)[k]], pair(zs[(0, 4, 3, 5, 1, 7, 2, 6)[k]], 1 - c, 1 - y))
    logits_of(0, other_lanes)
    logits_of(1, other_lanes)
    triple = end(triple, st_in, tickets)
    tickets = begin(triple, tot_mine, tot_in, column)
    logits_of(2, other_lanes)
    logits_of(3, other_lanes)
    other_marked = marks(other_lanes)
    row_top, row_total, row_named = end(triple, tot_in, tickets)
    log_total = row_top + jnp.log(row_total)
    lt_mine[0:4] = log_total
    lt_mine[4:8] = jnp.zeros((4, 128), F32)
    lt_ticket = send(lt_mine, lt_in, near_y[0])

    factor = LOSS_SCALE * jnp.exp(top - unfold(log_total))

    def own_grads(k, _):
        at_k = pl.ds(pl.multiple_of(k * 128, 128), 128)
        code_at = lax.broadcasted_iota(jnp.int32, (128, R), 0) + k * 128
        grad = lg[at_k, own_lanes] * factor - jnp.where(code_at == marked, LOSS_SCALE, 0.0)
        gt[at_k, own_lanes] = grad.astype(BF16)
        g[:, at_k] = grad.T.astype(BF16)
        return 0

    lax.fori_loop(0, VD // 128, own_grads, 0)

    def core_rows(cc):
        return pl.ds(pl.multiple_of(cc * 256, 256), 256)

    def theirs(k, _):
        at_k = pl.ds(pl.multiple_of(k * 512, 512), 512)
        hd_out[:, at_k] = nn(g[core_rows(1 - c), :], w[:, at_k]).astype(BF16)
        return 0

    lax.fori_loop(0, D // 512, theirs, 0)
    d_ticket = send(hd_out, hd_in, other_c)

    arrive(lt_ticket, lt_in)
    other_total = unfold(lt_in[0:4])

    def other_grads(k, _):
        at_k = pl.ds(pl.multiple_of(k * 128, 128), 128)
        code_at = lax.broadcasted_iota(jnp.int32, (128, R), 0) + k * 128
        grad = jnp.exp(lg[at_k, other_lanes] - other_total)
        grad = LOSS_SCALE * (grad - jnp.where(code_at == other_marked, 1.0, 0.0))
        gt[at_k, other_lanes] = grad.astype(BF16)
        return 0

    lax.fori_loop(0, VD // 128, other_grads, 0)

    def part(chunk, xx):
        start, size = chunk
        at_s = pl.ds(pl.multiple_of((y * 4 + xx) * CW, CW), CW)
        return nn(gt[start : start + size, :], hx[:, at_s])

    def halves_of(chunk):
        start, size = chunk
        return slice(start, start + size // 2), slice(start + size // 2, start + size)

    a_tickets, lr_tickets = [], []
    for chunk in CHUNKS:
        start, size = chunk
        xs[0, start : start + size, :] = part(chunk, far_x).astype(BF16)
        a_tickets.append([
            send(xs.at[0, spot], xa_in.at[spot], at(xx=to))
            for spot, to in zip(halves_of(chunk), (right_x, left_x))
        ])

    arrive(d_ticket, hd_in)

    def ours(k, _):
        at_k = pl.ds(pl.multiple_of(k * 512, 512), 512)
        hacc[:, at_k] = nn(g[core_rows(c), :], w[:, at_k]) + hd_in[:, at_k].astype(F32)
        return 0

    lax.fori_loop(0, D // 512, ours, 0)

    def owner_rows(k, hh):
        return pl.ds(pl.multiple_of(zs[k] * 32 + hh * 16, 16), 16)

    h_tickets = []
    for first, last in GROUPS:
        for slot in range(first, last):
            yo[slot] = hacc[owner_rows(FAR[slot], 1 - h), :].astype(BF16)
        h_tickets.append(send(yo.at[first:last], yi.at[first:last], other_h))

    z_tickets = {}

    def along_z(group):
        first, last = GROUPS[group]
        arrive(h_tickets[group], yi.at[first:last])
        for slot in range(first, last):
            k = FAR[slot]
            if k:
                zo[slot] = (hacc[owner_rows(k, h), :] + yi[slot].astype(F32)).astype(BF16)
                z_tickets[slot] = send(zo.at[slot], zi.at[slot], at(zz=zs[k]))

    for k, chunk in enumerate(CHUNKS):
        start, size = chunk
        sides = []
        for side, (to, into) in enumerate(((right_x, xl_in), (left_x, xr_in))):
            value = part(chunk, to)
            spot = halves_of(chunk)[side]
            arrive(a_tickets[k][side], xa_in.at[spot])
            near = xa_in[spot, :].astype(F32)
            half = size // 2
            if side == 0:
                value = jnp.concatenate([value[:half] + near, value[half:]], axis=0)
            else:
                value = jnp.concatenate([value[:half], value[half:] + near], axis=0)
            xs[1 + side, start : start + size, :] = value.astype(BF16)
            sides.append(send(
                xs.at[1 + side, start : start + size], into.at[start : start + size], at(xx=to)
            ))
        lr_tickets.append(sides)
        along_z(k)

    loss_mine[0:4] = log_total - row_named
    lanes8 = lax.broadcasted_iota(jnp.int32, (4, 128), 1)
    sends = jnp.zeros((4, 128), F32)
    for j in range(NS):
        sends = jnp.where(lanes8 == j, counts[0, 0, j].astype(F32), sends)
    loss_mine[4:8] = sends
    loss_tickets = [send(loss_mine, loss_in.at[k], device) for k, device in enumerate(others)]

    for k, chunk in enumerate(CHUNKS):
        start, size = chunk
        spot = slice(start, start + size)
        value = part(chunk, x)
        arrive(lr_tickets[k][0], xl_in.at[spot])
        arrive(lr_tickets[k][1], xr_in.at[spot])
        value = value + xl_in[spot, :].astype(F32) + xr_in[spot, :].astype(F32)
        code_out[spot, :] = value.astype(BF16)

    own = hacc[owner_rows(0, h), :] + yi[7].astype(F32)
    for slot in range(7):
        arrive(z_tickets[slot], zi.at[slot])
        own = own + zi[slot].astype(F32)
    spread = position((2 * RD, RD), 1) == lax.broadcasted_iota(jnp.int32, (2 * RD, RD), 0)
    hid_out[...] = nn(spread.astype(F32).astype(BF16), own.astype(BF16)).astype(BF16)

    tiles = [loss_mine[...]]
    for k, ticket in enumerate(loss_tickets):
        arrive(ticket, loss_in.at[k])
        tiles.append(loss_in[k])
    lane1 = lax.broadcasted_iota(jnp.int32, (1, 128), 1)
    own_row = lax.broadcasted_iota(jnp.int32, (4, 128), 0) == (c * 2 + z // 4)
    rank = lane1 - (lax.rem(z, 4) * 32 + h * 16)
    in_block = (rank >= 0) & (rank < RD)
    slots = lax.broadcasted_iota(jnp.int32, (RD, 128), 0)
    got, before, losses = [], [], []
    for tile in tiles:
        row = tile[4:5]
        got.append(jnp.sum(jnp.where(lane1 == me_s, row, 0.0), axis=1, keepdims=True).astype(jnp.int32))
        before.append(jnp.sum(jnp.where(lane1 < me_s, row, 0.0), axis=1, keepdims=True).astype(jnp.int32))
        losses.append(jnp.sum(jnp.where(own_row, tile[0:4], 0.0), axis=0, keepdims=True))
    listed = jnp.zeros((RD, 128), F32)
    for k in range(NS):
        source = lax.rem(me_s + NS - k, NS)
        first = jnp.zeros((1, 1), jnp.int32)
        for j in range(NS):
            earlier = lax.rem(me_s + NS - j, NS) < source
            first = first + jnp.where(earlier, got[j], 0)
        offset = rank - before[k]
        live = in_block & (offset >= 0) & (offset < got[k])
        slot = jnp.where(live, first + offset, -1)
        listed = listed + jnp.where(slots == slot, losses[k], 0.0)
    loss_out[...] = listed

    for copy in sent:
        copy.wait_send()


def per_device(hidden, head_weight, targets, span_counts, send_counts):
    vmem, smem = pl.BlockSpec(memory_space=pltpu.VMEM), pl.BlockSpec(memory_space=pltpu.SMEM)
    copies = 160
    code_grad, hidden_grad, listed = pl.pallas_call(
        body,
        out_shape=(
            jax.ShapeDtypeStruct((VD, CW), BF16),
            jax.ShapeDtypeStruct((2 * RD, D), BF16),
            jax.ShapeDtypeStruct((RD, 128), F32),
        ),
        in_specs=[smem, smem, smem, vmem, pl.BlockSpec(memory_space=pl.ANY)],
        out_specs=(vmem, vmem, vmem),
        scratch_shapes=[
            pltpu.VMEM((VD, D), BF16),
            pltpu.VMEM((2 * R, HX), BF16),
            pltpu.VMEM((VD, 2 * R), F32),
            pltpu.VMEM((VD, 2 * R), BF16),
            pltpu.VMEM((R, VD), BF16),
            pltpu.VMEM((16, 128), F32),
            pltpu.VMEM((3, 16, 128), F32),
            pltpu.VMEM((16, 128), F32),
            pltpu.VMEM((7, 16, 128), F32),
            pltpu.VMEM((8, 128), F32),
            pltpu.VMEM((8, 128), F32),
            pltpu.VMEM((8, 128), F32),
            pltpu.VMEM((7, 8, 128), F32),
            pltpu.VMEM((3, VD, CW), BF16),
            pltpu.VMEM((VD, CW), BF16),
            pltpu.VMEM((VD, CW), BF16),
            pltpu.VMEM((VD, CW), BF16),
            pltpu.VMEM((256, D), BF16),
            pltpu.VMEM((256, D), BF16),
            pltpu.VMEM((256, D), F32),
            pltpu.VMEM((8, RD, D), BF16),
            pltpu.VMEM((8, RD, D), BF16),
            pltpu.VMEM((7, RD, D), BF16),
            pltpu.VMEM((7, RD, D), BF16),
            pltpu.SemaphoreType.DMA((copies,)),
            pltpu.SemaphoreType.DMA((copies,)),
            pltpu.SemaphoreType.DMA,
        ],
        compiler_params=pltpu.CompilerParams(
            collective_id=0, has_side_effects=True, vmem_limit_bytes=56 * 1024 * 1024
        ),
        name="head",
    )(span_counts, send_counts, targets, hidden, head_weight)
    return (
        jnp.sum(listed, axis=1).reshape(1, 1, RD),
        hidden_grad.reshape(hidden.shape),
        code_grad,
    )


def solution(mesh):
    in_specs = (
        P("seq", "vocab", None, None, None),
        P("vocab", None),
        P("seq", "vocab", None, None),
        P("seq", "vocab", None),
        P("seq", "vocab", None),
    )
    out_specs = (P("seq", "vocab", None), P("seq", "vocab", None, None, None), P("vocab", "seq"))
    return jax.shard_map(
        per_device, mesh=mesh, in_specs=in_specs, out_specs=out_specs, check_vma=False
    )
```

time: 93.7 us -> 79.4 us (0.85)
  the two profiles are of different devices: /device:TPU:32 before, /device:TPU:1 now
where the time goes in v2:
time: 79.4 us; the launch traced here: 79.2 us
  Pallas kernels  73.8 us (93%)
  local copies, waits for them, and re-layouts  3.43 us (4%)
  other arithmetic  1.32 us (2%)
    pallas_call x1, Pallas kernels, per_device(): pl.pallas_call(body, out_shape=(jax.ShapeDtypeStruct((VD, CW), BF16), jax...  73.8 us
    unnamed x2, local copies, waits for them, and re-layouts  3.43 us

profile of v2, /device:TPU:1, one launch (start us, length us, event | category | flops | bytes accessed | tf_op | source)
XLA Modules:
  0.0 79.2 jit_solution(13057758502145785373)
XLA Ops:
  0.6 73.8 %head.1 = (bf16[1024,256]{1,0:T(8,128)(2,1)}, bf16[32,2048]{1,0:T(8,128)(2,1)}, f32[16,128]{1,0:T(8,128)}) custom-call(s32[1,1,2]{2,1,0:T(1,128)} %spans.1, s32[1,1,8]{2,1,0:T(1,128)} %counts.1, s32[1,1,2,16]{3,2,1,0:T(2,128)} %targets.1, bf16[1,1,2,16,2048]{4,3,2,1,0:T(8,128)(2,1)} %hidden.1, bf16[1024,2048]{1,0:T(8,128)(2,1)} %weight.1), custom_call_target="tpu_custom_call" | custom-call | tf_op jit(solution)/shard_map/head/pallas_call | solution.py:413
  74.5 1.3 %reduce_sum.9 = f32[16]{0:T(128)} reduce(f32[16,128]{1,0:T(8,128)} %get-tuple-element.6, f32[]{:T(128)} %constant.0.clone.1), dimensions={1}, to_apply=%region_0.0 | reduce | flops 2032 | bytes 8260 | tf_op jit(solution)/shard_map/reduce_sum | solution.py:457
  75.8 1.6 %copy.10 = bf16[1,1,2,16,2048]{4,3,2,1,0:T(8,128)(2,1)} copy(bf16[1,1,2,16,2048]{4,3,2,1,0:T(8,128)(2,1)} %bitcast.2) | data formatting | bytes 262144
  77.4 1.9 %copy.11 = bf16[1024,256]{1,0:T(8,128)(2,1)} copy(bf16[1024,256]{1,0:T(8,128)(2,1)} %get-tuple-element.14) | data formatting | bytes 1048576

commit v3 on v2

--- a/solution.py
+++ b/solution.py
@@ -17,8 +17,8 @@
 CW = D // NS
 HX = D + 128
 CHUNKS = [(256 * k, 256) for k in range(4)]
-FAR = (4, 3, 5, 2, 6, 1, 7, 0)
-GROUPS = ((0, 1), (1, 3), (3, 5), (5, 8))
+FAR = (4, 3, 5, 2, 6)
+GROUPS = ((0, 1), (1, 3), (3, 5))
 F32, BF16 = jnp.float32, jnp.bfloat16
 MESH = pl.DeviceIdType.MESH
 
@@ -32,13 +32,13 @@
 
 
 def body(
-    spans, counts, targets, hidden, weight,
+    spans, counts, targets, hidden_at, weight,
     code_out, hid_out, loss_out,
     w, hx, lg, gt, g,
     st_mine, st_in, tot_mine, tot_in, lt_mine, lt_in, loss_mine, loss_in,
     xs, xa_in, xl_in, xr_in,
-    hd_out, hd_in, hacc, yo, yi, zo, zi,
-    ssem, rsem, wsem,
+    hd_out, hd_in, hacc, yo, yi, zo, zi, zp_out, zp_in,
+    hidden, ssem, rsem, wsem,
 ):
     me_s, me_v = lax.axis_index("seq"), lax.axis_index("vocab")
     x, y = lax.rem(me_s, 4), me_s // 4
@@ -81,11 +81,13 @@
     ]
     peers = layer + column + others + near_y[1:]
 
-    weight_in = pltpu.make_async_copy(weight, w, wsem)
-    weight_in.start()
     barrier = pltpu.get_barrier_semaphore()
     for device in peers:
         pl.semaphore_signal(barrier, inc=1, device_id=device, device_id_type=MESH)
+    hidden_in = pltpu.make_async_copy(hidden_at, hidden, wsem.at[0])
+    hidden_in.start()
+    weight_in = pltpu.make_async_copy(weight, w, wsem.at[1])
+    weight_in.start()
 
     s0 = spans[0, 0, 0]
 
@@ -94,6 +96,7 @@
         return jnp.where(rank < s0, RD - s0 + rank, RD + rank)
 
     pick = position((RD, 2 * RD), 0) == lax.broadcasted_iota(jnp.int32, (RD, 2 * RD), 1)
+    hidden_in.wait()
     packed = nn(pick.astype(F32).astype(BF16), hidden[0, 0].reshape(2 * RD, D)).astype(BF16)
     place = position((RD, 128), 0)
     code = jnp.zeros((RD, 128), jnp.int32)
@@ -176,7 +179,7 @@
     own_crossed, crossed = crossed, {}
     for k in range(4):
         logits_of(k, own_lanes)
-        for kk in ((0, 4), (3, 5), (1, 7), (2, 6))[k]:
+        for kk in ((0, 1), (7, 2), (6, 4), (3, 5))[k]:
             for device, hh in zip(near_y, (h, 1 - h)):
                 ticket = by_y[kk][0 if device is near_y[0] else 1]
                 arrive(ticket, block(zs[kk], hh, 1 - y))
@@ -234,7 +237,7 @@
     triple = tuple(fold(row) for row in (top, total, named))
     tickets = begin(triple, st_mine, st_in, layer)
     for k in range(8):
-        arrive(crossed[(0, 4, 3, 5, 1, 7, 2, 6)[k]], pair(zs[(0, 4, 3, 5, 1, 7, 2, 6)[k]], 1 - c, 1 - y))
+        arrive(crossed[k], pair(zs[k], 1 - c, 1 - y))
     logits_of(0, other_lanes)
     logits_of(1, other_lanes)
     triple = end(triple, st_in, tickets)
@@ -314,6 +317,10 @@
     def owner_rows(k, hh):
         return pl.ds(pl.multiple_of(zs[k] * 32 + hh * 16, 16), 16)
 
+    p_tickets = []
+    for i, k in enumerate((1, 7)):
+        zp_out[i] = hacc[pl.ds(pl.multiple_of(zs[k] * 32, 32), 32), :].astype(BF16)
+        p_tickets.append(send(zp_out.at[i], zp_in.at[i], at(zz=zs[k])))
     h_tickets = []
     for first, last in GROUPS:
         for slot in range(first, last):
@@ -327,9 +334,12 @@
         arrive(h_tickets[group], yi.at[first:last])
         for slot in range(first, last):
             k = FAR[slot]
-            if k:
-                zo[slot] = (hacc[owner_rows(k, h), :] + yi[slot].astype(F32)).astype(BF16)
-                z_tickets[slot] = send(zo.at[slot], zi.at[slot], at(zz=zs[k]))
+            zo[slot] = (hacc[owner_rows(k, h), :] + yi[slot].astype(F32)).astype(BF16)
+            z_tickets[slot] = send(zo.at[slot], zi.at[slot], at(zz=zs[k]))
+
+    def near_sum(hh):
+        at_h = pl.ds(pl.multiple_of(hh * 16, 16), 16)
+        return hacc[owner_rows(0, hh), :] + zp_in[0, at_h, :].astype(F32) + zp_in[1, at_h, :].astype(F32)
 
     for k, chunk in enumerate(CHUNKS):
         start, size = chunk
@@ -349,7 +359,13 @@
                 xs.at[1 + side, start : start + size], into.at[start : start + size], at(xx=to)
             ))
         lr_tickets.append(sides)
-        along_z(k)
+        if k < 3:
+            along_z(k)
+        if k == 1:
+            for i, ticket in enumerate(p_tickets):
+                arrive(ticket, zp_in.at[i])
+            yo[5] = near_sum(1 - h).astype(BF16)
+            near_ticket = send(yo.at[5], yi.at[5], other_h)
 
     loss_mine[0:4] = log_total - row_named
     lanes8 = lax.broadcasted_iota(jnp.int32, (4, 128), 1)
@@ -368,8 +384,9 @@
         value = value + xl_in[spot, :].astype(F32) + xr_in[spot, :].astype(F32)
         code_out[spot, :] = value.astype(BF16)
 
-    own = hacc[owner_rows(0, h), :] + yi[7].astype(F32)
-    for slot in range(7):
+    arrive(near_ticket, yi.at[5])
+    own = near_sum(h) + yi[5].astype(F32)
+    for slot in range(5):
         arrive(z_tickets[slot], zi.at[slot])
         own = own + zi[slot].astype(F32)
     spread = position((2 * RD, RD), 1) == lax.broadcasted_iota(jnp.int32, (2 * RD, RD), 0)
@@ -401,7 +418,8 @@
         live = in_block & (offset >= 0) & (offset < got[k])
         slot = jnp.where(live, first + offset, -1)
         listed = listed + jnp.where(slots == slot, losses[k], 0.0)
-    loss_out[...] = listed
+    turned = jnp.concatenate([listed, jnp.zeros((128 - RD, 128), F32)], axis=0).T
+    loss_out[0] = jnp.sum(turned, axis=0, keepdims=True)[:, 0:RD]
 
     for copy in sent:
         copy.wait_send()
@@ -413,11 +431,11 @@
     code_grad, hidden_grad, listed = pl.pallas_call(
         body,
         out_shape=(
-            jax.ShapeDtypeStruct((VD, CW), BF16),
-            jax.ShapeDtypeStruct((2 * RD, D), BF16),
-            jax.ShapeDtypeStruct((RD, 128), F32),
+            pltpu.VMEM((VD, CW), BF16),
+            pltpu.VMEM((2 * RD, D), BF16),
+            pltpu.VMEM((1, 1, RD), F32),
         ),
-        in_specs=[smem, smem, smem, vmem, pl.BlockSpec(memory_space=pl.ANY)],
+        in_specs=[smem, smem, smem, pl.BlockSpec(memory_space=pl.ANY), pl.BlockSpec(memory_space=pl.ANY)],
         out_specs=(vmem, vmem, vmem),
         scratch_shapes=[
             pltpu.VMEM((VD, D), BF16),
@@ -440,24 +458,40 @@
             pltpu.VMEM((256, D), BF16),
             pltpu.VMEM((256, D), BF16),
             pltpu.VMEM((256, D), F32),
-            pltpu.VMEM((8, RD, D), BF16),
-            pltpu.VMEM((8, RD, D), BF16),
-            pltpu.VMEM((7, RD, D), BF16),
-            pltpu.VMEM((7, RD, D), BF16),
+            pltpu.VMEM((6, RD, D), BF16),
+            pltpu.VMEM((6, RD, D), BF16),
+            pltpu.VMEM((5, RD, D), BF16),
+            pltpu.VMEM((5, RD, D), BF16),
+            pltpu.VMEM((2, 2 * RD, D), BF16),
+            pltpu.VMEM((2, 2 * RD, D), BF16),
+            pltpu.VMEM((1, 1, 2, RD, D), BF16),
             pltpu.SemaphoreType.DMA((copies,)),
             pltpu.SemaphoreType.DMA((copies,)),
-            pltpu.SemaphoreType.DMA,
+            pltpu.SemaphoreType.DMA((2,)),
         ],
         compiler_params=pltpu.CompilerParams(
             collective_id=0, has_side_effects=True, vmem_limit_bytes=56 * 1024 * 1024
         ),
         name="head",
     )(span_counts, send_counts, targets, hidden, head_weight)
-    return (
-        jnp.sum(listed, axis=1).reshape(1, 1, RD),
-        hidden_grad.reshape(hidden.shape),
-        code_grad,
-    )
+    code_grad, hidden_grad, losses = pl.pallas_call(
+        hand_over,
+        out_shape=(
+            jax.ShapeDtypeStruct((VD, CW), BF16),
+            jax.ShapeDtypeStruct((2 * RD, D), BF16),
+            jax.ShapeDtypeStruct((1, 1, RD), F32),
+        ),
+        in_specs=[vmem] * 3,
+        out_specs=(vmem,) * 3,
+        name="hand_over",
+    )(*(pltpu.with_memory_space_constraint(a, pltpu.VMEM) for a in (code_grad, hidden_grad, listed)))
+    return losses, hidden_grad.reshape(hidden.shape), code_grad
+
+
+def hand_over(code_in, hid_in, loss_in, code_out, hid_out, loss_out):
+    code_out[...] = code_in[...]
+    hid_out[...] = hid_in[...]
+    loss_out[...] = loss_in[...]
 
 
 def solution(mesh):

time: 79.4 us -> 74 us (0.932)
  local copies, waits for them, and re-layouts: 3.43 us -> 0 us
  other arithmetic: 1.32 us -> 0 us
    unnamed x2 -> x0, local copies, waits for them, and re-layouts: 3.43 us -> none
    reduce_sum x1 -> x0, other arithmetic: 1.32 us -> none  [per_device(): jnp.sum(listed, axis=1).reshape(1, 1, RD)]
    pallas_call x1 -> x2, Pallas kernels: 73.8 us -> 73.3 us  [the longest x1 72.4 us: per_device(): pl.pallas_call(body, out_shape=(pltpu.VMEM((VD, CW), BF16), pltpu.VMEM((2...]
where the time goes in v3:
time: 74 us; the launch traced here: 73.9 us
  Pallas kernels  73.3 us (99%)
    pallas_call x1, Pallas kernels, per_device(): pl.pallas_call(body, out_shape=(pltpu.VMEM((VD, CW), BF16), pltpu.VMEM((2...  72.4 us

profile of v3, /device:TPU:1, one launch (start us, length us, event | category | flops | bytes accessed | tf_op | source)
XLA Modules:
  0.0 73.9 jit_solution(12644064398015228879)
XLA Ops:
  0.6 72.4 %head.1 = (bf16[1024,256]{1,0:T(8,128)(2,1)S(1)}, bf16[32,2048]{1,0:T(8,128)(2,1)S(1)}, f32[1,1,16]{2,1,0:T(1,128)S(1)}) custom-call(s32[1,1,2]{2,1,0:T(1,128)} %spans.1, s32[1,1,8]{2,1,0:T(1,128)} %counts.1, s32[1,1,2,16]{3,2,1,0:T(2,128)} %targets.1, bf16[1,1,2,16,2048]{4,3,2,1,0:T(8,128)(2,1)} %hidden_at.1, bf16[1024,2048]{1,0:T(8,128)(2,1)} %weight.1), custom_call_target="tpu_custom_call" | custom-call | tf_op jit(solution)/shard_map/head/pallas_call | solution.py:431
  73.0 0.9 %hand_over.1 = (bf16[1024,256]{1,0:T(8,128)(2,1)}, bf16[32,2048]{1,0:T(8,128)(2,1)}, f32[1,1,16]{2,1,0:T(1,128)}) custom-call(bf16[1024,256]{1,0:T(8,128)(2,1)S(1)} %get-tuple-element.9.code_in, bf16[32,2048]{1,0:T(8,128)(2,1)S(1)} %get-tuple-element.10.hid_in, f32[1,1,16]{2,1,0:T(1,128)S(1)} %get-tuple-element.11.loss_in), custom_call_target="tpu_custom_call" | custom-call | tf_op jit(solution)/shard_map/hand_over/pallas_call | solution.py:477

commit v4 on v3

--- a/solution.py
+++ b/solution.py
@@ -35,9 +35,9 @@
     spans, counts, targets, hidden_at, weight,
     code_out, hid_out, loss_out,
     w, hx, lg, gt, g,
-    st_mine, st_in, tot_mine, tot_in, lt_mine, lt_in, loss_mine, loss_in,
+    fc, st_mine, st_in, tot_mine, tot_in, loss_mine, loss_in,
     xs, xa_in, xl_in, xr_in,
-    hd_out, hd_in, hacc, yo, yi, zo, zi, zp_out, zp_in,
+    x_own, code_own, ha, hd_out, hd_in, hacc, yo, yi, zo, zi, zp_out, zp_in,
     hidden, ssem, rsem, wsem,
 ):
     me_s, me_v = lax.axis_index("seq"), lax.axis_index("vocab")
@@ -75,17 +75,18 @@
     other_c, other_h = at(cc=1 - c), at(hh=1 - h)
     near_y = [at(yy=1 - y), at(yy=1 - y, hh=1 - h)]
     layer = [other_c, other_h, at(hh=1 - h, cc=1 - c)]
-    column = [at(zz=zs[k]) for k in range(1, 8)]
+    column = [at(zz=zs[k]) for k in (4, 3, 5, 2, 6, 1, 7)]
     others = [
         {"seq": lax.rem(me_s + k, NS), "vocab": me_v} for k in range(1, NS)
     ]
-    peers = layer + column + others + near_y[1:]
-
+    across = [at(yy=1 - y, zz=zs[k]) for k in (4, 3, 5, 2, 6, 1, 7, 0)]
+    peers = layer + column + others + near_y[1:] + across[:7]
+
+    hidden_in = pltpu.make_async_copy(hidden_at, hidden, wsem.at[0])
+    hidden_in.start()
     barrier = pltpu.get_barrier_semaphore()
     for device in peers:
         pl.semaphore_signal(barrier, inc=1, device_id=device, device_id_type=MESH)
-    hidden_in = pltpu.make_async_copy(hidden_at, hidden, wsem.at[0])
-    hidden_in.start()
     weight_in = pltpu.make_async_copy(weight, w, wsem.at[1])
     weight_in.start()
 
@@ -173,17 +174,20 @@
     other_lanes = pl.ds(pl.multiple_of((1 - y) * R, R), R)
 
     def logits_of(k, lanes):
-        at_k = slice(256 * k, 256 * (k + 1))
+        at_k = slice(512 * k, 512 * (k + 1))
         lg[at_k, lanes] = nt(w[at_k, :], hx[lanes, 0:D])
 
-    own_crossed, crossed = crossed, {}
-    for k in range(4):
+    crossed = {}
+
+    def take_other(k):
+        for ticket, hh in zip(by_y[k], (h, 1 - h)):
+            arrive(ticket, block(zs[k], hh, 1 - y))
+        cross(k, 1 - y)
+
+    for k in range(2):
         logits_of(k, own_lanes)
-        for kk in ((0, 1), (7, 2), (6, 4), (3, 5))[k]:
-            for device, hh in zip(near_y, (h, 1 - h)):
-                ticket = by_y[kk][0 if device is near_y[0] else 1]
-                arrive(ticket, block(zs[kk], hh, 1 - y))
-            cross(kk, 1 - y)
+        for kk in ((0, 1, 7), (2, 6))[k]:
+            take_other(kk)
 
     ones = lax.broadcasted_iota(jnp.int32, (8, 128), 0) == lax.broadcasted_iota(jnp.int32, (8, 128), 1)
     ones = ones.astype(F32).astype(BF16)
@@ -196,17 +200,18 @@
     top = jnp.max(lg[:, own_lanes], axis=0, keepdims=True)
 
     def sums_of(k, carry):
-        total, named = carry
+        total, named, share = carry
         at_k = pl.ds(pl.multiple_of(k * 64, 64), 64)
         part = lg[at_k, own_lanes]
-        code_at = lax.broadcasted_iota(jnp.int32, (64, R), 0) + k * 64
-        named = named + jnp.sum(jnp.where(code_at == marked, part, 0.0), axis=0, keepdims=True)
+        hit = lax.broadcasted_iota(jnp.int32, (64, R), 0) + k * 64 == marked
+        named = named + jnp.sum(jnp.where(hit, part, 0.0), axis=0, keepdims=True)
         grown = jnp.exp(part - top)
         lg[at_k, own_lanes] = grown
-        return total + jnp.sum(grown, axis=0, keepdims=True), named
-
-    total, named = lax.fori_loop(
-        0, VD // 64, sums_of, (jnp.zeros((1, R), F32), jnp.zeros((1, R), F32))
+        share = share + jnp.sum(jnp.where(hit, grown, 0.0), axis=0, keepdims=True)
+        return total + jnp.sum(grown, axis=0, keepdims=True), named, share
+
+    total, named, share = lax.fori_loop(
+        0, VD // 64, sums_of, tuple(jnp.zeros((1, R), F32) for _ in range(3))
     )
 
     def fold(row):
@@ -234,59 +239,73 @@
             parts.append((in_ref[k, 0:4], in_ref[k, 4:8], in_ref[k, 8:12]))
         return join(*zip(*parts))
 
+    def core_lanes(cc):
+        return pl.ds(pl.multiple_of(y * R + cc * 256, 256), 256)
+
     triple = tuple(fold(row) for row in (top, total, named))
     tickets = begin(triple, st_mine, st_in, layer)
+    for k in (4, 3, 5):
+        take_other(k)
+
+    code_row = hx[core_lanes(1 - c), D:HX].astype(F32)
+    code_row = code_row[:, 0:1] * 256.0 + code_row[:, 1:2] - (me_v * VD).astype(F32)
+    their_marks = marks(core_lanes(1 - c))
+
+    def unnamed(k, _):
+        at_k = pl.ds(pl.multiple_of(k * 128, 128), 128)
+        code_at = lax.broadcasted_iota(jnp.int32, (128, 256), 0) + k * 128
+        grown = jnp.where(code_at == their_marks, 0.0, lg[at_k, core_lanes(1 - c)])
+        g[0:256, at_k] = grown.T.astype(BF16)
+        code_at = lax.broadcasted_iota(jnp.int32, (256, 128), 1) + k * 128
+        g[256:512, at_k] = (code_at.astype(F32) == code_row).astype(F32).astype(BF16)
+        return 0
+
+    lax.fori_loop(0, VD // 128, unnamed, 0)
     for k in range(8):
         arrive(crossed[k], pair(zs[k], 1 - c, 1 - y))
     logits_of(0, other_lanes)
+    triple = end(triple, st_in, tickets)
+    tickets = begin(triple, tot_mine, tot_in, column + across)
     logits_of(1, other_lanes)
-    triple = end(triple, st_in, tickets)
-    tickets = begin(triple, tot_mine, tot_in, column)
-    logits_of(2, other_lanes)
-    logits_of(3, other_lanes)
     other_marked = marks(other_lanes)
-    row_top, row_total, row_named = end(triple, tot_in, tickets)
+
+    def theirs(k, _):
+        at_k = pl.ds(pl.multiple_of(k * 512, 512), 512)
+        ha[:, at_k] = nn(g[...], w[:, at_k])
+        return 0
+
+    lax.fori_loop(0, D // 512, theirs, 0)
+    row_top, row_total, row_named = end(triple, tot_in, tickets[:7])
     log_total = row_top + jnp.log(row_total)
-    lt_mine[0:4] = log_total
-    lt_mine[4:8] = jnp.zeros((4, 128), F32)
-    lt_ticket = send(lt_mine, lt_in, near_y[0])
 
     factor = LOSS_SCALE * jnp.exp(top - unfold(log_total))
-
-    def own_grads(k, _):
+    both = jnp.concatenate([factor, factor * share - LOSS_SCALE, jnp.zeros((126, R), F32)], axis=0)
+    fc[...] = jnp.where(c == 0, both[:, 256:512], both[:, 0:256]).T
+
+    d_tickets = []
+    for k in range(4):
+        at_k = slice(512 * k, 512 * (k + 1))
+        hd_out[k] = (fc[:, 0:1] * ha[0:256, at_k] + fc[:, 1:2] * ha[256:512, at_k]).astype(BF16)
+        d_tickets.append(send(hd_out.at[k], hd_in.at[k], other_c))
+
+    other_parts = []
+    for k, ticket in enumerate(tickets[7:]):
+        arrive(ticket, tot_in.at[7 + k])
+        other_parts.append((tot_in[7 + k, 0:4], tot_in[7 + k, 4:8], tot_in[7 + k, 8:12]))
+    other_top, other_sum, _ = join(*zip(*other_parts))
+    other_total = unfold(other_top + jnp.log(other_sum))
+
+    def grads_of(k, _):
         at_k = pl.ds(pl.multiple_of(k * 128, 128), 128)
         code_at = lax.broadcasted_iota(jnp.int32, (128, R), 0) + k * 128
         grad = lg[at_k, own_lanes] * factor - jnp.where(code_at == marked, LOSS_SCALE, 0.0)
         gt[at_k, own_lanes] = grad.astype(BF16)
-        g[:, at_k] = grad.T.astype(BF16)
-        return 0
-
-    lax.fori_loop(0, VD // 128, own_grads, 0)
-
-    def core_rows(cc):
-        return pl.ds(pl.multiple_of(cc * 256, 256), 256)
-
-    def theirs(k, _):
-        at_k = pl.ds(pl.multiple_of(k * 512, 512), 512)
-        hd_out[:, at_k] = nn(g[core_rows(1 - c), :], w[:, at_k]).astype(BF16)
-        return 0
-
-    lax.fori_loop(0, D // 512, theirs, 0)
-    d_ticket = send(hd_out, hd_in, other_c)
-
-    arrive(lt_ticket, lt_in)
-    other_total = unfold(lt_in[0:4])
-
-    def other_grads(k, _):
-        at_k = pl.ds(pl.multiple_of(k * 128, 128), 128)
-        code_at = lax.broadcasted_iota(jnp.int32, (128, R), 0) + k * 128
+        g[0:256, at_k] = jnp.where(c == 0, grad[:, 0:256], grad[:, 256:512]).T.astype(BF16)
         grad = jnp.exp(lg[at_k, other_lanes] - other_total)
         grad = LOSS_SCALE * (grad - jnp.where(code_at == other_marked, 1.0, 0.0))
         gt[at_k, other_lanes] = grad.astype(BF16)
         return 0
 
-    lax.fori_loop(0, VD // 128, other_grads, 0)
-
     def part(chunk, xx):
         start, size = chunk
         at_s = pl.ds(pl.multiple_of((y * 4 + xx) * CW, CW), CW)
@@ -299,20 +318,18 @@
     a_tickets, lr_tickets = [], []
     for chunk in CHUNKS:
         start, size = chunk
+        lax.fori_loop(start // 128, (start + size) // 128, grads_of, 0)
         xs[0, start : start + size, :] = part(chunk, far_x).astype(BF16)
         a_tickets.append([
             send(xs.at[0, spot], xa_in.at[spot], at(xx=to))
             for spot, to in zip(halves_of(chunk), (right_x, left_x))
         ])
 
-    arrive(d_ticket, hd_in)
-
-    def ours(k, _):
-        at_k = pl.ds(pl.multiple_of(k * 512, 512), 512)
-        hacc[:, at_k] = nn(g[core_rows(c), :], w[:, at_k]) + hd_in[:, at_k].astype(F32)
-        return 0
-
-    lax.fori_loop(0, D // 512, ours, 0)
+    for k, ticket in enumerate(d_tickets):
+        at_k = slice(512 * k, 512 * (k + 1))
+        ours = nn(g[0:256, :], w[:, at_k])
+        arrive(ticket, hd_in.at[k])
+        hacc[:, at_k] = ours + hd_in[k].astype(F32)
 
     def owner_rows(k, hh):
         return pl.ds(pl.multiple_of(zs[k] * 32 + hh * 16, 16), 16)
@@ -341,31 +358,41 @@
         at_h = pl.ds(pl.multiple_of(hh * 16, 16), 16)
         return hacc[owner_rows(0, hh), :] + zp_in[0, at_h, :].astype(F32) + zp_in[1, at_h, :].astype(F32)
 
+    sides = ((right_x, xl_in), (left_x, xr_in))
     for k, chunk in enumerate(CHUNKS):
-        start, size = chunk
-        sides = []
-        for side, (to, into) in enumerate(((right_x, xl_in), (left_x, xr_in))):
+        spots, half = halves_of(chunk), chunk[1] // 2
+        tickets = []
+        for side, (to, into) in enumerate(sides):
             value = part(chunk, to)
-            spot = halves_of(chunk)[side]
+            joined, plain = value[:half], value[half:]
+            if side:
+                joined, plain = plain, joined
+            x_own[side, half * k : half * (k + 1), :] = joined
+            spot = spots[1 - side]
+            xs[1 + side, spot, :] = plain.astype(BF16)
+            tickets.append((send(xs.at[1 + side, spot], into.at[spot], at(xx=to)), into.at[spot]))
+        lr_tickets.append(tickets)
+        if k == 1:
+            along_z(0)
+
+    for k, chunk in enumerate(CHUNKS):
+        spots, half = halves_of(chunk), chunk[1] // 2
+        for side, (to, into) in enumerate(sides):
+            spot = spots[side]
             arrive(a_tickets[k][side], xa_in.at[spot])
-            near = xa_in[spot, :].astype(F32)
-            half = size // 2
-            if side == 0:
-                value = jnp.concatenate([value[:half] + near, value[half:]], axis=0)
-            else:
-                value = jnp.concatenate([value[:half], value[half:] + near], axis=0)
-            xs[1 + side, start : start + size, :] = value.astype(BF16)
-            sides.append(send(
-                xs.at[1 + side, start : start + size], into.at[start : start + size], at(xx=to)
-            ))
-        lr_tickets.append(sides)
-        if k < 3:
-            along_z(k)
+            value = x_own[side, half * k : half * (k + 1), :] + xa_in[spot, :].astype(F32)
+            xs[1 + side, spot, :] = value.astype(BF16)
+            ticket = send(xs.at[1 + side, spot], into.at[spot], at(xx=to))
+            lr_tickets[k].append((ticket, into.at[spot]))
+        if k == 0:
+            along_z(1)
         if k == 1:
             for i, ticket in enumerate(p_tickets):
                 arrive(ticket, zp_in.at[i])
             yo[5] = near_sum(1 - h).astype(BF16)
             near_ticket = send(yo.at[5], yi.at[5], other_h)
+        if k == 2:
+            along_z(2)
 
     loss_mine[0:4] = log_total - row_named
     lanes8 = lax.broadcasted_iota(jnp.int32, (4, 128), 1)
@@ -375,23 +402,12 @@
     loss_mine[4:8] = sends
     loss_tickets = [send(loss_mine, loss_in.at[k], device) for k, device in enumerate(others)]
 
-    for k, chunk in enumerate(CHUNKS):
+    for _ in range(len(sent) - 20):
+        sent.pop(0).wait_send()
+
+    for chunk in CHUNKS:
         start, size = chunk
-        spot = slice(start, start + size)
-        value = part(chunk, x)
-        arrive(lr_tickets[k][0], xl_in.at[spot])
-        arrive(lr_tickets[k][1], xr_in.at[spot])
-        value = value + xl_in[spot, :].astype(F32) + xr_in[spot, :].astype(F32)
-        code_out[spot, :] = value.astype(BF16)
-
-    arrive(near_ticket, yi.at[5])
-    own = near_sum(h) + yi[5].astype(F32)
-    for slot in range(5):
-        arrive(z_tickets[slot], zi.at[slot])
-        own = own + zi[slot].astype(F32)
-    spread = position((2 * RD, RD), 1) == lax.broadcasted_iota(jnp.int32, (2 * RD, RD), 0)
-    hid_out[...] = nn(spread.astype(F32).astype(BF16), own.astype(BF16)).astype(BF16)
-
+        code_own[start : start + size, :] = part(chunk, x)
     tiles = [loss_mine[...]]
     for k, ticket in enumerate(loss_tickets):
         arrive(ticket, loss_in.at[k])
@@ -421,13 +437,30 @@
     turned = jnp.concatenate([listed, jnp.zeros((128 - RD, 128), F32)], axis=0).T
     loss_out[0] = jnp.sum(turned, axis=0, keepdims=True)[:, 0:RD]
 
+    for k, chunk in enumerate(CHUNKS):
+        start, size = chunk
+        spot = slice(start, start + size)
+        value = code_own[spot, :]
+        for ticket, where in lr_tickets[k]:
+            arrive(ticket, where)
+        value = value + xl_in[spot, :].astype(F32) + xr_in[spot, :].astype(F32)
+        code_out[spot, :] = value.astype(BF16)
+
+    arrive(near_ticket, yi.at[5])
+    own = near_sum(h) + yi[5].astype(F32)
+    for slot in range(5):
+        arrive(z_tickets[slot], zi.at[slot])
+        own = own + zi[slot].astype(F32)
+    spread = position((2 * RD, RD), 1) == lax.broadcasted_iota(jnp.int32, (2 * RD, RD), 0)
+    hid_out[...] = nn(spread.astype(F32).astype(BF16), own.astype(BF16)).astype(BF16)
+
     for copy in sent:
         copy.wait_send()
 
 
 def per_device(hidden, head_weight, targets, span_counts, send_counts):
     vmem, smem = pl.BlockSpec(memory_space=pltpu.VMEM), pl.BlockSpec(memory_space=pltpu.SMEM)
-    copies = 160
+    copies = 192
     code_grad, hidden_grad, listed = pl.pallas_call(
         body,
         out_shape=(
@@ -442,21 +475,23 @@
             pltpu.VMEM((2 * R, HX), BF16),
             pltpu.VMEM((VD, 2 * R), F32),
             pltpu.VMEM((VD, 2 * R), BF16),
-            pltpu.VMEM((R, VD), BF16),
+            pltpu.VMEM((512, VD), BF16),
+            pltpu.VMEM((256, 128), F32),
             pltpu.VMEM((16, 128), F32),
             pltpu.VMEM((3, 16, 128), F32),
             pltpu.VMEM((16, 128), F32),
-            pltpu.VMEM((7, 16, 128), F32),
-            pltpu.VMEM((8, 128), F32),
-            pltpu.VMEM((8, 128), F32),
+            pltpu.VMEM((15, 16, 128), F32),
             pltpu.VMEM((8, 128), F32),
             pltpu.VMEM((7, 8, 128), F32),
             pltpu.VMEM((3, VD, CW), BF16),
             pltpu.VMEM((VD, CW), BF16),
             pltpu.VMEM((VD, CW), BF16),
             pltpu.VMEM((VD, CW), BF16),
-            pltpu.VMEM((256, D), BF16),
-            pltpu.VMEM((256, D), BF16),
+            pltpu.VMEM((2, VD // 2, CW), F32),
+            pltpu.VMEM((VD, CW), F32),
+            pltpu.VMEM((512, D), F32),
+            pltpu.VMEM((4, 256, 512), BF16),
+            pltpu.VMEM((4, 256, 512), BF16),
             pltpu.VMEM((256, D), F32),
             pltpu.VMEM((6, RD, D), BF16),
             pltpu.VMEM((6, RD, D), BF16),

time: 74 us -> 71.5 us (0.966)
  the two profiles are of different devices: /device:TPU:1 before, /device:TPU:32 now
where the time goes in v4:
time: 71.5 us; the launch traced here: 71.2 us
  Pallas kernels  70.5 us (99%)
    pallas_call x1, Pallas kernels, per_device(): pl.pallas_call(body, out_shape=(pltpu.VMEM((VD, CW), BF16), pltpu.VMEM((2...  69.7 us

profile of v4, /device:TPU:32, one launch (start us, length us, event | category | flops | bytes accessed | tf_op | source)
XLA Modules:
  0.0 71.2 jit_solution(426041057166376413)
XLA Ops:
  0.6 69.7 %head.1 = (bf16[1024,256]{1,0:T(8,128)(2,1)S(1)}, bf16[32,2048]{1,0:T(8,128)(2,1)S(1)}, f32[1,1,16]{2,1,0:T(1,128)S(1)}) custom-call(s32[1,1,2]{2,1,0:T(1,128)} %spans.1, s32[1,1,8]{2,1,0:T(1,128)} %counts.1, s32[1,1,2,16]{3,2,1,0:T(2,128)} %targets.1, bf16[1,1,2,16,2048]{4,3,2,1,0:T(8,128)(2,1)} %hidden_at.1, bf16[1024,2048]{1,0:T(8,128)(2,1)} %weight.1), custom_call_target="tpu_custom_call" | custom-call | tf_op jit(solution)/shard_map/head/pallas_call | solution.py:464
  70.3 0.9 %hand_over.1 = (bf16[1024,256]{1,0:T(8,128)(2,1)}, bf16[32,2048]{1,0:T(8,128)(2,1)}, f32[1,1,16]{2,1,0:T(1,128)}) custom-call(bf16[1024,256]{1,0:T(8,128)(2,1)S(1)} %get-tuple-element.9.code_in, bf16[32,2048]{1,0:T(8,128)(2,1)S(1)} %get-tuple-element.10.hid_in, f32[1,1,16]{2,1,0:T(1,128)S(1)} %get-tuple-element.11.loss_in), custom_call_target="tpu_custom_call" | custom-call | tf_op jit(solution)/shard_map/hand_over/pallas_call | solution.py:512

commit v5 on v4

--- a/solution.py
+++ b/solution.py
@@ -147,7 +147,6 @@
         spread_y(k)
     for k in (1, 7):
         arrive(by_z[k], block(zs[k], h))
-        spread_y(k)
     here = block(zs[7], 1 - h)
     arrive(ups, here)
     ups = send(here, here, up)
@@ -156,6 +155,11 @@
     arrive(downs, here)
     downs = send(here, here, down)
     cross(1)
+    for ticket, hh in zip(by_y[0], (h, 1 - h)):
+        arrive(ticket, block(z, hh, 1 - y))
+    theirs0 = pair(z, c, 1 - y)
+    by_zz = {7: send(theirs0, theirs0, up), 1: send(theirs0, theirs0, down)}
+    first_other = send(theirs0, theirs0, other_c)
     for k in (2, 6):
         arrive(by_z[k], block(zs[k], h))
         spread_y(k)
@@ -177,16 +181,19 @@
         at_k = slice(512 * k, 512 * (k + 1))
         lg[at_k, lanes] = nt(w[at_k, :], hx[lanes, 0:D])
 
-    crossed = {}
+    crossed = {0: first_other}
 
     def take_other(k):
-        for ticket, hh in zip(by_y[k], (h, 1 - h)):
-            arrive(ticket, block(zs[k], hh, 1 - y))
+        if k in (1, 7):
+            arrive(by_zz[k], pair(zs[k], c, 1 - y))
+        else:
+            for ticket, hh in zip(by_y[k], (h, 1 - h)):
+                arrive(ticket, block(zs[k], hh, 1 - y))
         cross(k, 1 - y)
 
     for k in range(2):
         logits_of(k, own_lanes)
-        for kk in ((0, 1, 7), (2, 6))[k]:
+        for kk in ((), ())[k]:
             take_other(kk)
 
     ones = lax.broadcasted_iota(jnp.int32, (8, 128), 0) == lax.broadcasted_iota(jnp.int32, (8, 128), 1)
@@ -244,7 +251,7 @@
 
     triple = tuple(fold(row) for row in (top, total, named))
     tickets = begin(triple, st_mine, st_in, layer)
-    for k in (4, 3, 5):
+    for k in (1, 7, 2, 6, 4, 3, 5):
         take_other(k)
 
     code_row = hx[core_lanes(1 - c), D:HX].astype(F32)

time: 71.5 us -> 69.7 us (0.975)
  Pallas kernels: 70.5 us -> 69 us
    pallas_call x1, Pallas kernels: 69.7 us -> 68.1 us  [per_device(): pl.pallas_call(body, out_shape=(pltpu.VMEM((VD, CW), BF16), pltpu.VMEM((2...]
where the time goes in v5:
time: 69.7 us; the launch traced here: 69.6 us
  Pallas kernels  69 us (99%)
    pallas_call x1, Pallas kernels, per_device(): pl.pallas_call(body, out_shape=(pltpu.VMEM((VD, CW), BF16), pltpu.VMEM((2...  68.1 us

profile of v5, /device:TPU:32, one launch (start us, length us, event | category | flops | bytes accessed | tf_op | source)
XLA Modules:
  0.0 69.6 jit_solution(6747474850903519048)
XLA Ops:
  0.6 68.1 %head.1 = (bf16[1024,256]{1,0:T(8,128)(2,1)S(1)}, bf16[32,2048]{1,0:T(8,128)(2,1)S(1)}, f32[1,1,16]{2,1,0:T(1,128)S(1)}) custom-call(s32[1,1,2]{2,1,0:T(1,128)} %spans.1, s32[1,1,8]{2,1,0:T(1,128)} %counts.1, s32[1,1,2,16]{3,2,1,0:T(2,128)} %targets.1, bf16[1,1,2,16,2048]{4,3,2,1,0:T(8,128)(2,1)} %hidden_at.1, bf16[1024,2048]{1,0:T(8,128)(2,1)} %weight.1), custom_call_target="tpu_custom_call" | custom-call | tf_op jit(solution)/shard_map/head/pallas_call | solution.py:471
  68.7 0.9 %hand_over.1 = (bf16[1024,256]{1,0:T(8,128)(2,1)}, bf16[32,2048]{1,0:T(8,128)(2,1)}, f32[1,1,16]{2,1,0:T(1,128)}) custom-call(bf16[1024,256]{1,0:T(8,128)(2,1)S(1)} %get-tuple-element.9.code_in, bf16[32,2048]{1,0:T(8,128)(2,1)S(1)} %get-tuple-element.10.hid_in, f32[1,1,16]{2,1,0:T(1,128)S(1)} %get-tuple-element.11.loss_in), custom_call_target="tpu_custom_call" | custom-call | tf_op jit(solution)/shard_map/hand_over/pallas_call | solution.py:519

commit v6 on v5

--- a/solution.py
+++ b/solution.py
@@ -144,6 +144,7 @@
         here = block(zs[k], h)
         arrive(by_z[k], here)
         by_h[k] = send(here, here, other_h)
+    for k in (4, 3, 5):
         spread_y(k)
     for k in (1, 7):
         arrive(by_z[k], block(zs[k], h))
@@ -193,8 +194,6 @@
 
     for k in range(2):
         logits_of(k, own_lanes)
-        for kk in ((), ())[k]:
-            take_other(kk)
 
     ones = lax.broadcasted_iota(jnp.int32, (8, 128), 0) == lax.broadcasted_iota(jnp.int32, (8, 128), 1)
     ones = ones.astype(F32).astype(BF16)

time: 69.7 us -> 69.7 us (level)
  no operation moved by 1% of the time
where the time goes in v6:
time: 69.7 us; the launch traced here: 69.6 us
  Pallas kernels  69 us (99%)
    pallas_call x1, Pallas kernels, per_device(): pl.pallas_call(body, out_shape=(pltpu.VMEM((VD, CW), BF16), pltpu.VMEM((2...  68.1 us

profile of v6, /device:TPU:32, one launch (start us, length us, event | category | flops | bytes accessed | tf_op | source)
XLA Modules:
  0.0 69.6 jit_solution(16811657232524343017)
XLA Ops:
  0.6 68.1 %head.1 = (bf16[1024,256]{1,0:T(8,128)(2,1)S(1)}, bf16[32,2048]{1,0:T(8,128)(2,1)S(1)}, f32[1,1,16]{2,1,0:T(1,128)S(1)}) custom-call(s32[1,1,2]{2,1,0:T(1,128)} %spans.1, s32[1,1,8]{2,1,0:T(1,128)} %counts.1, s32[1,1,2,16]{3,2,1,0:T(2,128)} %targets.1, bf16[1,1,2,16,2048]{4,3,2,1,0:T(8,128)(2,1)} %hidden_at.1, bf16[1024,2048]{1,0:T(8,128)(2,1)} %weight.1), custom_call_target="tpu_custom_call" | custom-call | tf_op jit(solution)/shard_map/head/pallas_call | solution.py:470
  68.7 0.9 %hand_over.1 = (bf16[1024,256]{1,0:T(8,128)(2,1)}, bf16[32,2048]{1,0:T(8,128)(2,1)}, f32[1,1,16]{2,1,0:T(1,128)}) custom-call(bf16[1024,256]{1,0:T(8,128)(2,1)S(1)} %get-tuple-element.9.code_in, bf16[32,2048]{1,0:T(8,128)(2,1)S(1)} %get-tuple-element.10.hid_in, f32[1,1,16]{2,1,0:T(1,128)S(1)} %get-tuple-element.11.loss_in), custom_call_target="tpu_custom_call" | custom-call | tf_op jit(solution)/shard_map/hand_over/pallas_call | solution.py:518
